TPU v7x, 32 devices: a whole 2x2x4 slice. The times are simulated.
32 devices in a mesh: cfg: 2 (over y), row: 4 (over z), col: 2 (over x), spin: 2 (over core).
Axes of the slice: x: 2, y: 2, z: 4, core: 2. Of those that a mesh axis runs over, the one named last changes fastest.
Arguments:
- perambulator: float32 [2, 8192, 4096], P(None, ('cfg', 'row'), ('col', 'spin')), parts along dimension 1, may hold values from -1 to 1
- insertion_ops: float32 [2, 2, 64, 64], replicated, may hold values from -0.75 to 0.75
- ins_times: int32 [2], replicated, may hold values from 0 to 15
- sign_table: int32 [2, 4], replicated, may hold values from 0 to 3
- perm_table: int32 [2, 4], replicated, may hold values from 0 to 3, each once within a row
Outputs:
- generalized: float32 [2, 8192, 4096], P(None, ('cfg', 'row'), ('col', 'spin')), parts along dimension 1
There are 2 independent parts, one for each index of `cfg`. A program takes and returns all parts, laid end to end along the dimension named above; an argument that names none is the same for every part. Nothing has to cross between parts.
All inputs are finite; a program needn't handle non-finite values.
Results may differ from a plain program's by a relative error of at most 0.0001.
Values sent between devices are 32-bit elements; how exact they have to be, the bound alone decides.
No kernel may reach another device: no remote copies, remote signals or barrier semaphores. Data moves between devices by JAX's collectives and lax.ppermute only.
A program may use at most 64 MiB of HBM per device.

v0:
```python
import jax
import jax.numpy as jnp
from jax import lax
from jax.sharding import PartitionSpec as P


def spread(value, axis, root):
    mine = lax.axis_index(axis) == root
    return lax.psum(jnp.where(mine, value, jnp.zeros_like(value)), axis)


def complex_product(former_real, former_imag, latter_real, latter_imag, product):
    first_term = product(former_real, latter_real)
    second_term = product(former_imag, latter_imag)
    third_term = product(former_real + former_imag, latter_real + latter_imag)
    return (first_term - second_term, third_term - first_term - second_term)


def matrix_product(former, latter):
    return jnp.dot(former, latter, precision=lax.Precision.HIGHEST)


def spin_product(former, latter):
    return jnp.einsum("ab,sbc->sac", former, latter, precision=lax.Precision.HIGHEST)


def mix_spins(row_slab, op_real, op_imag):
    vec_count = op_real.shape[0]
    col_count = row_slab.shape[2]
    slab_real = row_slab[0].reshape(-1, vec_count, col_count)
    slab_imag = row_slab[1].reshape(-1, vec_count, col_count)
    combined_real, combined_imaginary = complex_product(
        op_real, op_imag, slab_real, slab_imag, spin_product
    )
    return jnp.stack(
        [combined_real.reshape(-1, col_count), combined_imaginary.reshape(-1, col_count)]
    )


def permute_signs(mixed, sign_row, perm_row, vec_count):
    col_count = mixed.shape[2]
    spin_count = sign_row.shape[0]
    combined_real = mixed[0].reshape(spin_count, vec_count, col_count)
    combined_imaginary = mixed[1].reshape(spin_count, vec_count, col_count)
    selected_real = jnp.zeros_like(combined_real)
    selected_imaginary = jnp.zeros_like(combined_imaginary)
    for source_spin in range(spin_count):
        weight_col = (perm_row == source_spin).astype(jnp.float32)[:, None, None]
        selected_real = selected_real + weight_col * combined_real[source_spin][None]
        selected_imaginary = selected_imaginary + weight_col * combined_imaginary[source_spin][None]
    phase_factor_real = ((sign_row == 0).astype(jnp.float32) - (sign_row == 2).astype(jnp.float32))[
        :, None, None
    ]
    phase_imag = ((sign_row == 1).astype(jnp.float32) - (sign_row == 3).astype(jnp.float32))[
        :, None, None
    ]
    out_real = phase_factor_real * selected_real - phase_imag * selected_imaginary
    out_imag = phase_factor_real * selected_imaginary + phase_imag * selected_real
    return (out_real.reshape(-1, col_count), out_imag.reshape(-1, col_count))


def shards(perambulator, insertion_ops, ins_times, sign_table, perm_table):
    vec_count = insertion_ops.shape[2]
    block_order = sign_table.shape[1] * vec_count
    row_count = perambulator.shape[1]
    col_count = perambulator.shape[2]
    piece_rows = min(block_order, row_count)
    piece_count = block_order // piece_rows
    times_local = col_count // block_order
    running = jnp.zeros((2, row_count, col_count), jnp.float32)
    for ins_index in range(insertion_ops.shape[0]):
        moment = ins_times[ins_index]
        op_real = insertion_ops[ins_index, 0]
        op_imag = insertion_ops[ins_index, 1]
        column_local = lax.dynamic_slice_in_dim(
            perambulator, moment % times_local * block_order, block_order, 2
        )
        column = spread(column_local, ("col", "spin"), moment // times_local)
        received = []
        for piece_index in range(piece_count):
            start_row = moment * block_order + piece_index * piece_rows
            candidate = lax.dynamic_slice_in_dim(perambulator, start_row % row_count, piece_rows, 1)
            received.append(spread(candidate, "row", start_row // row_count))
        row_slab = jnp.concatenate(received, axis=1) if piece_count > 1 else received[0]
        mixed = mix_spins(row_slab, op_real, op_imag)
        inserted_real, inserted_imag = permute_signs(
            mixed, sign_table[ins_index], perm_table[ins_index], vec_count
        )
        part_real, part_imag = complex_product(
            column[0], column[1], inserted_real, inserted_imag, matrix_product
        )
        running = running + jnp.stack([part_real, part_imag])
    return running


def solution(mesh):
    return jax.shard_map(
        shards,
        mesh=mesh,
        in_specs=(P(None, ("cfg", "row"), ("col", "spin")), P(), P(), P(), P()),
        out_specs=P(None, ("cfg", "row"), ("col", "spin")),
        check_vma=False,
    )
```

profile of v0, /device:TPU:0, one launch (start us, length us, event | category | flops | bytes accessed | tf_op | source)
XLA Modules:
  0.0 300.7 jit_solution(9227453074744381797)
XLA Ops:
  6.5 1.3 fusion.58
  9.3 5.1 %dynamic-slice_select_fusion = (f32[2,256,1024]{2,1,0:T(8,128)}, f32[2,256,1024]{2,1,0:T(8,128)}) fusion(f32[2,1024,1024]{2,1,0:T(8,128)} %param.5, s32[]{:T(128)S(6)} %select_n.90, pred[]{:T(512)S(6)} %eq.159, s32[]{:T(128)S(6)} %select_n.80, pred[]{:T(512)S(6)} %eq.149), kind=kLoop, calls=%fused_computation.5 | loop fusion | flops 1048576 | bytes 8388618 | tf_op jit(solution)/shard_map/jit(_where)/select_n | solution.py:9
  19.7 4.7 %dynamic-slice_select_fusion.1 = (f32[2,1024,256]{2,1,0:T(8,128)}, f32[2,1024,256]{2,1,0:T(8,128)}) fusion(f32[2,1024,1024]{2,1,0:T(8,128)} %param.5, s32[]{:T(128)S(6)} %select_n.85, pred[]{:T(512)S(6)} %eq.155, s32[]{:T(128)S(6)} %select_n.75, pred[]{:T(512)S(6)} %eq.145), kind=kLoop, calls=%fused_computation.6 | loop fusion | flops 1048576 | bytes 8388618 | tf_op jit(solution)/shard_map/jit(_where)/select_n | solution.py:9
  25.1 147.5 %all-reduce.7.cloned.1.call-done = (f32[2,256,1024]{2,1,0:T(8,128)}, f32[2,256,1024]{2,1,0:T(8,128)}) async-done(((f32[2,256,1024]{2,1,0:T(8,128)}, f32[2,256,1024]{2,1,0:T(8,128)}), (f32[2,256,1024]{2,1,0:T(8,128)}, f32[2,256,1024]{2,1,0:T(8,128)})) %all-reduce.7.cloned.1.call-update) | async-done | bytes 4194320 | tf_op jit(solution)/shard_map/psum | solution.py:9
  172.5 3.0 slice_add_fusion
  175.5 1.1 convolution_bitcast_fusion.4
  176.6 1.3 fusion.59
  178.0 1.3 fusion.3
  179.2 0.9 slice_bitcast_fusion.15
  180.1 1.0 slice_bitcast_fusion.11
  181.1 1.1 convolution_bitcast_fusion.1
  182.2 1.3 fusion.60
  183.6 1.3 fusion.1
  185.0 0.8 fusion.56
  185.8 74.0 %all-reduce.5.cloned.1.call-done = (f32[2,1024,256]{2,1,0:T(8,128)}, f32[2,1024,256]{2,1,0:T(8,128)}) async-done(((f32[2,1024,256]{2,1,0:T(8,128)}, f32[2,1024,256]{2,1,0:T(8,128)}), (f32[2,1024,256]{2,1,0:T(8,128)}, f32[2,1024,256]{2,1,0:T(8,128)})) %all-reduce.5.cloned.1.call-update) | async-done | bytes 4194320 | tf_op jit(solution)/shard_map/psum | solution.py:9
  259.9 5.3 %fusion.7 = f32[1024,1024]{1,0:T(8,128)S(1)} fusion(f32[256,1024]{1,0:T(8,128)S(1)} %bitcast.171, f32[2,1024,256]{2,1,0:T(8,128)} %get-tuple-element.6), kind=kOutput, calls=%fused_computation.22 | convolution fusion | flops 3221225472 | bytes 6291456 | tf_op jit(solution)/shard_map/dot_general | solution.py:20
  265.2 3.8 %fusion.5 = f32[1024,1024]{1,0:T(8,128)S(1)} fusion(f32[256,1024]{1,0:T(8,128)S(1)} %bitcast.170, f32[2,1024,256]{2,1,0:T(8,128)S(1)} %copy-done.1), kind=kOutput, calls=%fused_computation.20 | convolution fusion | flops 3221225472 | bytes 6291456 | tf_op jit(solution)/shard_map/dot_general | solution.py:20
  269.0 1.4 subtract_bitcast_fusion.1
  270.4 4.2 %subtract_bitcast_fusion = f32[1,1024,1024]{2,1,0:T(8,128)S(1)} fusion(f32[1024,1024]{1,0:T(8,128)S(1)} %fusion.5, f32[1024,1024]{1,0:T(8,128)S(1)} %fusion.7, f32[256,1024]{1,0:T(8,128)S(1)} %bitcast.162, f32[2,1024,256]{2,1,0:T(8,128)S(1)} %copy-done.1), kind=kOutput, calls=%fused_computation.1 | convolution fusion | flops 3223584768 | bytes 15728640 | tf_op jit(solution)/shard_map/dot_general | solution.py:20
  276.2 4.0 %fusion.12 = f32[1024,1024]{1,0:T(8,128)S(1)} fusion(f32[256,1024]{1,0:T(8,128)S(1)} %bitcast.173, f32[2,1024,256]{2,1,0:T(8,128)S(1)} %copy-done), kind=kOutput, calls=%fused_computation.27 | convolution fusion | flops 3221225472 | bytes 6291456 | tf_op jit(solution)/shard_map/dot_general | solution.py:20
  280.2 3.7 %fusion.10 = f32[1024,1024]{1,0:T(8,128)S(1)} fusion(f32[256,1024]{1,0:T(8,128)S(1)} %bitcast.172, f32[2,1024,256]{2,1,0:T(8,128)S(1)} %copy-done), kind=kOutput, calls=%fused_computation.25 | convolution fusion | flops 3221225472 | bytes 6291456 | tf_op jit(solution)/shard_map/dot_general | solution.py:20
  283.9 1.4 subtract_bitcast_fusion.3
  285.3 4.2 %subtract_bitcast_fusion.2 = f32[1,1024,1024]{2,1,0:T(8,128)S(1)} fusion(f32[1024,1024]{1,0:T(8,128)S(1)} %fusion.10, f32[1024,1024]{1,0:T(8,128)S(1)} %fusion.12, f32[256,1024]{1,0:T(8,128)S(1)} %bitcast.163, f32[2,1024,256]{2,1,0:T(8,128)S(1)} %copy-done), kind=kOutput, calls=%fused_computation.3 | convolution fusion | flops 3223584768 | bytes 15728640 | tf_op jit(solution)/shard_map/dot_general | solution.py:20
  289.5 4.3 %maximum_add_fusion = f32[2,1024,1024]{2,1,0:T(8,128)} fusion(f32[1,1024,1024]{2,1,0:T(8,128)S(1)} %subtract_bitcast_fusion.2, f32[1,1024,1024]{2,1,0:T(8,128)S(1)} %subtract_bitcast_fusion.3, f32[1,1024,1024]{2,1,0:T(8,128)S(1)} %subtract_bitcast_fusion, f32[1,1024,1024]{2,1,0:T(8,128)S(1)} %subtract_bitcast_fusion.1), kind=kLoop, calls=%fused_computation | loop fusion | flops 6291456 | bytes 25165824 | tf_op jit(solution)/shard_map/add | solution.py:92
  (33 shorter events, 2.4 us)
Async XLA Ops:
  6.5 166.0 %all-reduce.7.cloned.1.call-start = ((), (), s32[]{:S(2)}) async-start(), calls=%async_computation.1 | async-start | bytes 8388608 | tf_op jit(solution)/shard_map/psum | solution.py:9
  14.4 245.5 %all-reduce.5.cloned.1.call-start = ((), (), s32[]{:S(2)}) async-start(), calls=%async_computation | async-start | bytes 8388608 | tf_op jit(solution)/shard_map/psum | solution.py:9
  24.4 0.7 copy-start.10
  24.4 0.7 copy-start.11
  172.5 3.0 copy-start.9
  259.9 5.3 %copy-start.1 = (f32[2,1024,256]{2,1,0:T(8,128)S(1)}, f32[2,1024,256]{2,1,0:T(8,128)}, u32[]{:S(2)}) copy-start(f32[2,1024,256]{2,1,0:T(8,128)} %get-tuple-element.6) | copy-start | bytes 6291460
  270.3 4.3 %copy-start.2 = (f32[64,1024]{1,0:T(8,128)S(1)}, f32[64,1024]{1,0:T(8,128)}, u32[]{:S(2)}) copy-start(f32[64,1024]{1,0:T(8,128)} %get-tuple-element.34) | copy-start | bytes 786436
  270.3 4.3 %copy-start.3 = (f32[64,1024]{1,0:T(8,128)S(1)}, f32[64,1024]{1,0:T(8,128)}, u32[]{:S(2)}) copy-start(f32[64,1024]{1,0:T(8,128)} %get-tuple-element.35) | copy-start | bytes 786436
  270.3 4.3 %copy-start.4 = (f32[64,1024]{1,0:T(8,128)S(1)}, f32[64,1024]{1,0:T(8,128)}, u32[]{:S(2)}) copy-start(f32[64,1024]{1,0:T(8,128)} %get-tuple-element.36) | copy-start | bytes 786436
  270.4 4.3 %copy-start.5 = (f32[64,1024]{1,0:T(8,128)S(1)}, f32[64,1024]{1,0:T(8,128)}, u32[]{:S(2)}) copy-start(f32[64,1024]{1,0:T(8,128)} %get-tuple-element.37) | copy-start | bytes 786436
  270.4 4.3 %copy-start.6 = (f32[64,1024]{1,0:T(8,128)S(1)}, f32[64,1024]{1,0:T(8,128)}, u32[]{:S(2)}) copy-start(f32[64,1024]{1,0:T(8,128)} %get-tuple-element.38) | copy-start | bytes 786436
  270.4 4.3 %copy-start.7 = (f32[64,1024]{1,0:T(8,128)S(1)}, f32[64,1024]{1,0:T(8,128)}, u32[]{:S(2)}) copy-start(f32[64,1024]{1,0:T(8,128)} %get-tuple-element.39) | copy-start | bytes 786436
  270.4 4.3 %copy-start.8 = (f32[64,1024]{1,0:T(8,128)S(1)}, f32[64,1024]{1,0:T(8,128)}, u32[]{:S(2)}) copy-start(f32[64,1024]{1,0:T(8,128)} %get-tuple-element.40) | copy-start | bytes 786436
  274.6 1.6 copy-start
Sparse Core Ops, SparseCore 0:
  14.5 158.0 all-reduce.6
  175.1 84.6 all-reduce.4
where the time goes:
time: 301 us
  waiting for transfers between devices  222 us (74%)
  matrix products  32.6 us (11%)
  other arithmetic  21.5 us (7%)
  between operations  20.3 us (7%)
  local copies, waits for them, and re-layouts  4.79 us (2%)
    psum x2, waiting for transfers between devices, spread(): return lax.psum(jnp.where(mine, value, jnp.zeros_like(value)), axis)  221 us
    dot_general x6, matrix products, matrix_product(): return jnp.dot(former, latter, precision=lax.Precision.HIGHEST)  25.2 us
    select_n x2, other arithmetic, spread(): return lax.psum(jnp.where(mine, value, jnp.zeros_like(value)), axis)  9.77 us
    dot_general x6, matrix products, spin_product(): jnp.einsum('ab,sbc->sac', former, latter, precision=lax.Precision.HIGHEST)  7.37 us
  transfers between devices with their start and end apart: 2, of which 2 were waited for; matrix products, arithmetic and copies ran while one was open for 6% of the time, Pallas kernels for 0%

commit v1 on v0

v1 whole, which is shorter than its diff:
```python
import functools

import jax
import jax.numpy as jnp
from jax import lax
from jax.experimental import pallas as pl
from jax.experimental.pallas import tpu as pltpu
from jax.sharding import PartitionSpec as P

VMEM_BYTES = 40 * 1024 * 1024
LINE = 4
PIECES = 8
GROUP = 2
MINE, COLUMNS, FOLD = 1, 5, 6
BLOCKS = {7: (0,), 8: (2,), 9: (4,)}


def split(value):
    upper = value.astype(jnp.bfloat16)
    lower = (value - upper.astype(jnp.float32)).astype(jnp.bfloat16)
    return upper, lower


def three_pass(a_upper, a_lower, b_upper, b_lower):
    def dot(a, b):
        return jnp.dot(a, b, preferred_element_type=jnp.float32)

    return dot(a_upper, b_upper) + (dot(a_upper, b_lower) + dot(a_lower, b_upper))


def fold_kernel(numbers, own_ref, other_ref, op_ref, upper_ref, lower_ref, g_upper, g_lower):
    stream, half = pl.program_id(0), pl.program_id(1)
    vec_count, order = op_ref.shape[2:]
    spins = order // vec_count
    insertion = jnp.where(numbers[1] == 1, 1 - stream, stream)

    @pl.when((half == 0) & (pl.program_id(2) == 0))
    def _():
        lane_spin = lax.broadcasted_iota(jnp.int32, (vec_count, order), 1) // vec_count
        op_real, op_imag = op_ref[insertion, 0], op_ref[insertion, 1]
        for spin in range(spins):
            sign = numbers[2 + insertion * spins + spin]
            column = numbers[2 + (2 + insertion) * spins + spin]
            hit = lane_spin == column
            odd = (sign == 1) | (sign == 3)
            flip = jnp.where(sign >= 2, -1.0, 1.0)
            real = jnp.where(hit, flip * jnp.where(odd, -op_imag, op_real), 0.0)
            imag = jnp.where(hit, flip * jnp.where(odd, op_real, op_imag), 0.0)
            real_parts, imag_parts = split(real), split(imag)
            first = pl.ds(spin * vec_count, vec_count)
            second = pl.ds(order + spin * vec_count, vec_count)
            for ref, part_real, part_imag in zip((g_upper, g_lower), real_parts, imag_parts):
                ref[first, :order] = part_real
                ref[first, order:] = part_imag
                ref[second, :order] = -part_imag
                ref[second, order:] = part_real

    mine = numbers[0] == half
    joined = jnp.concatenate(
        [
            jnp.where(mine, own_ref[0, 0], other_ref[0, 0]),
            jnp.where(mine, own_ref[0, 1], other_ref[0, 1]),
        ],
        axis=1,
    )
    product = three_pass(*split(joined), g_upper[...], g_lower[...])
    upper_ref[...], lower_ref[...] = split(product)


def fold(numbers, own, other, ops):
    streams, _, rows, order = own.shape
    tile = rows // 2
    shape = jax.ShapeDtypeStruct((2 * rows, streams * 2 * order), jnp.bfloat16)
    slab_spec = pl.BlockSpec((1, 2, tile, order), lambda k, h, i, numbers: (k, 0, i, 0))
    out_spec = pl.BlockSpec((tile, 2 * order), lambda k, h, i, numbers: (2 * h + i, k))
    return pl.pallas_call(
        fold_kernel,
        grid_spec=pltpu.PrefetchScalarGridSpec(
            num_scalar_prefetch=1,
            grid=(streams, 2, 2),
            in_specs=[
                slab_spec,
                slab_spec,
                pl.BlockSpec(ops.shape, lambda k, h, i, numbers: (0, 0, 0, 0)),
            ],
            out_specs=[out_spec, out_spec],
            scratch_shapes=[pltpu.VMEM((2 * order, 2 * order), jnp.bfloat16)] * 2,
        ),
        out_shape=[shape, shape],
        compiler_params=pltpu.CompilerParams(vmem_limit_bytes=VMEM_BYTES),
        cost_estimate=pl.CostEstimate(
            flops=24 * streams * 2 * rows * order * 2 * order,
            bytes_accessed=16 * own.size,
            transcendentals=0,
        ),
        name="fold",
    )(numbers, own, other, ops)


def block_kernel(upper_ref, lower_ref, *refs):
    out_ref, r_upper, r_lower = refs[-3:]
    order = refs[0].shape[1]
    part = refs[0].shape[2]
    width = GROUP * part

    @pl.when(pl.program_id(0) == 0)
    def _():
        for index, ref in enumerate(refs[: 2 * GROUP]):
            stream, piece = divmod(index, GROUP)
            first_rows = pl.ds(2 * stream * order, order)
            second_rows = pl.ds((2 * stream + 1) * order, order)
            first_lanes = pl.ds(piece * part, part)
            second_lanes = pl.ds(width + piece * part, part)
            for target, real, imag in zip((r_upper, r_lower), split(ref[0]), split(ref[1])):
                target[first_rows, first_lanes] = real
                target[first_rows, second_lanes] = imag
                target[second_rows, first_lanes] = -imag
                target[second_rows, second_lanes] = real

    product = three_pass(upper_ref[...], lower_ref[...], r_upper[...], r_lower[...])
    out_ref[0] = product[:, :width]
    out_ref[1] = product[:, width:]


def block(folded, first, chains, previous=None):
    upper, lower = folded
    row_count, depth = upper.shape
    order = depth // 4
    tile = row_count // 4
    pieces = [chain.piece(first + p) for chain in chains for p in range(GROUP)]
    part = pieces[0].shape[2]
    width = GROUP * part
    left = pl.BlockSpec((tile, depth), lambda i: (i, 0))
    whole = pl.BlockSpec((2, order, part), lambda i: (0, 0, 0))
    operands = [upper, lower] + pieces
    specs = [left, left] + [whole] * len(pieces)
    aliases = {}
    if previous is not None:
        aliases = {len(operands): 0}
        operands.append(previous)
        specs.append(pl.BlockSpec(memory_space=pl.ANY))
    place = first // GROUP
    return pl.pallas_call(
        block_kernel,
        grid=(row_count // tile,),
        in_specs=specs,
        out_specs=pl.BlockSpec((2, tile, width), lambda i: (0, i, place)),
        out_shape=jax.ShapeDtypeStruct((2, row_count, PIECES * part), jnp.float32),
        scratch_shapes=[pltpu.VMEM((depth, 2 * width), jnp.bfloat16)] * 2,
        input_output_aliases=aliases,
        compiler_params=pltpu.CompilerParams(vmem_limit_bytes=VMEM_BYTES),
        cost_estimate=pl.CostEstimate(
            flops=12 * row_count * depth * width,
            bytes_accessed=(4 * depth + 8 * width) * row_count,
            transcendentals=0,
        ),
        name="block",
    )(*operands)


def tie(value, *others):
    return lax.optimization_barrier((value,) + others)[0] if others else value


class Chain:
    def __init__(self, home, row, root, order):
        self.home, self.row, self.order = home, row, order
        self.width = home.shape[2] // PIECES
        place = lax.axis_index("row")
        self.outside = (place == 0) | (place == LINE - 1)
        self.holder = place == root
        beside = ((place == 1) & (root == 0)) | ((place == LINE - 2) & (root == LINE - 1))
        self.way = jnp.where(
            self.holder, 0, jnp.where(self.outside, 3, jnp.where(beside, 1, 2))
        )
        self.outer, self.inner = [], []
        slab = lax.dynamic_slice_in_dim(home, row, order, 1)
        self.own = lax.optimization_barrier(
            [
                lax.slice_in_dim(slab, p * self.width, (p + 1) * self.width, axis=2)
                for p in range(PIECES)
            ]
        )

    def step(self, index, *others):
        ahead = self.own[min(index, PIECES - 1)]
        if index:
            last = self.outer[-1:] + self.inner[-1:]
            ahead, *last = lax.optimization_barrier((ahead, *last, *others))[: 1 + len(last)]
            self.outer[-1] = last[0]
            if self.inner:
                self.inner[-1] = last[1]
        value = ahead
        if index >= 2:
            passing = jnp.where(self.holder, self.own[index - 2], self.inner[index - 2])
            value = jnp.where(self.outside, ahead, passing)
        if 1 <= index <= PIECES:
            crossing = jnp.where(self.holder, self.own[index - 1], self.outer[index - 1])
            self.inner.append(lax.ppermute(crossing, "row", [(1, 2), (2, 1)]))
        self.outer.append(lax.ppermute(value, "row", [(0, 1), (1, 0), (2, 3), (3, 2)]))

    def piece(self, index):
        value = self.outer[index + 2]
        for way, other in ((2, self.inner[index]), (1, self.outer[index]), (0, self.own[index])):
            value = jnp.where(self.way == way, other, value)
        return value


def planned(perambulator, insertion_ops, ins_times, sign_table, perm_table):
    vec_count = insertion_ops.shape[2]
    spins = sign_table.shape[1]
    order = spins * vec_count
    _, row_count, col_count = perambulator.shape
    rows_local = row_count // order
    times_local = col_count // order
    spin_size = lax.axis_size("spin")
    core, side = lax.axis_index("spin"), lax.axis_index("col")
    half_rows = row_count // 2
    exchange = [(0, 1), (1, 0)]

    chains = [
        Chain(
            perambulator,
            ins_times[k] % rows_local * order,
            ins_times[k] // rows_local,
            order,
        )
        for k in range(2)
    ]

    def columns(half):
        return jnp.stack(
            [
                lax.dynamic_slice(
                    perambulator,
                    (0, half * half_rows, ins_times[k] % times_local * order),
                    (2, half_rows, order),
                )
                for k in range(2)
            ]
        )

    owner = ins_times // times_local
    kept = columns(core)
    got = lax.ppermute(columns(1 - core), "spin", exchange)
    mine = jnp.where((owner % spin_size == core)[:, None, None, None], kept, got)
    across = lax.ppermute(mine, "col", exchange)
    settings = jnp.concatenate(
        [
            jnp.stack([core, 0]).astype(jnp.int32),
            sign_table.reshape(-1),
            perm_table.reshape(-1),
        ]
    )
    ops = jnp.tile(insertion_ops, (1, 1, 1, spins))

    result = None
    for index in range(PIECES + 2):
        before = ()
        if index == MINE:
            before = (mine,)
        elif index == COLUMNS:
            came = tie(across, *[chain.outer[-1] for chain in chains])
            chosen = jnp.where((owner // spin_size == side)[:, None, None, None], mine, came)
            before = (chosen,)
        elif index == FOLD:
            other = lax.ppermute(chosen, "spin", exchange)
            before = folded = fold(settings, chosen, other, ops)
        elif index in BLOCKS:
            for first in BLOCKS[index]:
                result = block(folded, first, chains, result)
            before = (result,)
        for chain in chains:
            chain.step(index, *before)
    return block(folded, PIECES - GROUP, chains, result)


def insertion_matrices(insertion_ops, sign_table, perm_table):
    spins = sign_table.shape[1]
    vec_count = insertion_ops.shape[2]
    order = spins * vec_count
    hit = perm_table[:, :, None] == jnp.arange(spins)[None, None, :]
    sign = sign_table[:, :, None]

    def weight(plus, minus):
        value = (sign == plus).astype(jnp.float32) - (sign == minus).astype(jnp.float32)
        return jnp.where(hit, value, 0.0)[:, :, None, :, None]

    real_weight, imag_weight = weight(0, 2), weight(1, 3)
    op_real = insertion_ops[:, 0][:, None, :, None, :]
    op_imag = insertion_ops[:, 1][:, None, :, None, :]
    real = (real_weight * op_real - imag_weight * op_imag).reshape(-1, order, order)
    imag = (real_weight * op_imag + imag_weight * op_real).reshape(-1, order, order)
    return jnp.concatenate(
        [jnp.concatenate([real, imag], axis=2), jnp.concatenate([-imag, real], axis=2)], axis=1
    )


def spread(value, axis, root):
    mine = lax.axis_index(axis) == root
    return lax.psum(jnp.where(mine, value, jnp.zeros_like(value)), axis)


def general(perambulator, insertion_ops, ins_times, sign_table, perm_table):
    vec_count = insertion_ops.shape[2]
    order = sign_table.shape[1] * vec_count
    _, row_count, col_count = perambulator.shape
    piece_rows = min(order, row_count)
    times_local = col_count // order
    gamma = insertion_matrices(insertion_ops, sign_table, perm_table)

    def dot(a, b):
        return jnp.dot(a, b, precision=lax.Precision.HIGHEST)

    real = imag = 0.0
    for k in range(insertion_ops.shape[0]):
        moment = ins_times[k]
        column = spread(
            lax.dynamic_slice_in_dim(perambulator, moment % times_local * order, order, 2),
            ("col", "spin"),
            moment // times_local,
        )
        received = []
        for piece in range(order // piece_rows):
            start = moment * order + piece * piece_rows
            candidate = lax.dynamic_slice_in_dim(perambulator, start % row_count, piece_rows, 1)
            received.append(spread(candidate, "row", start // row_count))
        slab = jnp.concatenate(received, axis=1)
        folded = dot(jnp.concatenate([column[0], column[1]], axis=1), gamma[k])
        left, right = folded[:, :order], folded[:, order:]
        real = real + dot(left, slab[0]) - dot(right, slab[1])
        imag = imag + dot(left, slab[1]) + dot(right, slab[0])
    return jnp.stack([real, imag])


def solution(mesh):
    def shards(perambulator, insertion_ops, ins_times, sign_table, perm_table):
        order = sign_table.shape[1] * insertion_ops.shape[2]
        fits = (
            mesh.shape["row"] == LINE
            and insertion_ops.shape[0] == 2
            and mesh.shape["col"] == 2
            and mesh.shape["spin"] == 2
            and perambulator.shape[1] % order == 0
        )
        arguments = (perambulator, insertion_ops, ins_times, sign_table, perm_table)
        return planned(*arguments) if fits else general(*arguments)

    return jax.shard_map(
        shards,
        mesh=mesh,
        in_specs=(P(None, ("cfg", "row"), ("col", "spin")), P(), P(), P(), P()),
        out_specs=P(None, ("cfg", "row"), ("col", "spin")),
        check_vma=False,
    )
```

time: 301 us -> 175 us (0.58)
  waiting for transfers between devices: 222 us -> 37 us
  starting transfers between devices: 0.04 us -> 73.7 us
  matrix products: 32.6 us -> 0 us
  Pallas kernels: 0 us -> 28.9 us
  between operations: 20.3 us -> 6.08 us
  local copies, waits for them, and re-layouts: 4.79 us -> 12.1 us
  other arithmetic: 21.5 us -> 16.1 us
    psum x2 -> x0, waiting for transfers between devices: 221 us -> none  [spread(): return lax.psum(jnp.where(mine, value, jnp.zeros_like(value)), axis)]
    ppermute x0 -> x39, starting transfers between devices: none -> 73.7 us  [the longest x20 59.3 us: step(): lax.ppermute(value, 'row', [(0, 1), (1, 0), (2, 3), (3, 2)])]
    ppermute x0 -> x39, waiting for transfers between devices: none -> 37 us  [the longest x20 34.7 us: step(): lax.ppermute(value, 'row', [(0, 1), (1, 0), (2, 3), (3, 2)])]
    dot_general x12 -> x0, matrix products: 32.6 us -> none  [the longest x6 25.2 us: matrix_product(): return jnp.dot(former, latter, precision=lax.Precision.HIGHEST)]
    pallas_call x0 -> x5, Pallas kernels: none -> 28.9 us  [the longest x4 20.4 us: block(): pl.pallas_call(block_kernel, grid=(row_count // tile,), in_specs=specs, o...]
    add x4 -> x0, other arithmetic: 8.96 us -> none  [the longest x3 4.61 us: complex_product(): third_term = product(former_real + former_imag, latter_real + latter_imag)]
    another operation x0 -> x3, local copies, waits for them, and re-layouts: none -> 4.95 us  [the longest x1 2.69 us: columns(): jnp.stack([lax.dynamic_slice(perambulator, (0, half * half_rows, ins_time...]
    select_n x2 -> x38, other arithmetic: 9.77 us -> 14.4 us  [the longest x11 5.82 us: step(): jnp.where(self.holder, self.own[index - 1], self.outer[index - 1])]
  transfers between devices with their start and end apart: 2 -> 39, of which waited for: 2 -> 13; matrix products, arithmetic and copies ran while one was open for 6% -> 11% of each run, Pallas kernels for 0% -> 14%
where the time goes in v1:
time: 175 us; the launch traced here: 174 us
  starting transfers between devices  73.7 us (42%)
  waiting for transfers between devices  37 us (21%)
  Pallas kernels  28.9 us (17%)
  other arithmetic  16.1 us (9%)
  local copies, waits for them, and re-layouts  12.1 us (7%)
  between operations  6.08 us (3%)
    ppermute x20, starting transfers between devices, step(): lax.ppermute(value, 'row', [(0, 1), (1, 0), (2, 3), (3, 2)])  59.3 us
    ppermute x20, waiting for transfers between devices, step(): lax.ppermute(value, 'row', [(0, 1), (1, 0), (2, 3), (3, 2)])  34.7 us
    pallas_call x4, Pallas kernels, block(): pl.pallas_call(block_kernel, grid=(row_count // tile,), in_specs=specs, o...  20.4 us
    ppermute x16, starting transfers between devices, step(): self.inner.append(lax.ppermute(crossing, 'row', [(1, 2), (2, 1)]))  12.3 us
    pallas_call x1, Pallas kernels, fold(): pl.pallas_call(fold_kernel, grid_spec=pltpu.PrefetchScalarGridSpec(num_sc...  8.54 us
    select_n x11, other arithmetic, step(): jnp.where(self.holder, self.own[index - 1], self.outer[index - 1])  5.82 us
    slice x1, local copies, waits for them, and re-layouts, __init__(): lax.slice_in_dim(slab, p * self.width, (p + 1) * self.width, axis=2)  3.86 us
  transfers between devices with their start and end apart: 39, of which 13 were waited for; matrix products, arithmetic and copies ran while one was open for 11% of the time, Pallas kernels for 14%

profile of v1, /device:TPU:0, one launch (start us, length us, event | category | flops | bytes accessed | tf_op | source)
XLA Modules:
  0.0 173.9 jit_solution(11962810363321823506)
XLA Ops:
  5.1 2.7 %dynamic-slice_bitcast_fusion.3 = (f32[1,2,512,256]{3,2,1,0:T(8,128)S(1)}, f32[1,2,512,256]{3,2,1,0:T(8,128)S(1)}, f32[1,2,512,256]{3,2,1,0:T(8,128)S(1)}, f32[1,2,512,256]{3,2,1,0:T(8,128)S(1)}) fusion(f32[2,1024,1024]{2,1,0:T(8,128)} %param.5, s32[]{:T(128)S(6)} %select_n.494, s32[]{:T(128)S(6)} %select_n.496, s32[]{:T(128)S(6)} %select_n.499, s32[]{:T(128)S(6)} %select_n.498), kind=kLoop, calls=%fused_computation.5 | loop fusion | bytes 8388624 | tf_op jit(solution)/shard_map/stack | solution.py:232
  9.9 3.9 %constant_dynamic-slice_fusion.14 = (f32[2,256,128]{2,1,0:T(8,128)S(1)}, f32[2,256,128]{2,1,0:T(8,128)}, f32[2,256,128]{2,1,0:T(8,128)}, f32[2,256,128]{2,1,0:T(...) fusion(f32[2,1024,1024]{2,1,0:T(8,128)} %param.5, ...), kind=kLoop, calls=%fused_computation.69 | loop fusion | bytes 8388644 | tf_op jit(solution)/shard_map/slice | solution.py:180
  17.3 3.2 %maximum_select_fusion = f32[2,2,512,256]{3,2,1,0:T(8,128)} fusion(f32[2,2,512,256]{3,2,1,0:T(8,128)} %collective-permute-done, f32[1,2,512,256]{3,2,1,0:T(8,128)S(1)} %get-tuple-element.168, f32[1,2,512,256]{3,2,1,0:T(8,128)S(1)} %get-tuple-element.165, pred[2]{0:T(512)(128)(4,1)S(1)} %fusion), kind=kLoop, calls=%fused_computation | loop fusion | flops 1048576 | bytes 6291458 | tf_op jit(solution)/shard_map/jit(_where)/select_n | solution.py:246
  20.5 3.4 %collective-permute-done.2 = f32[2,256,128]{2,1,0:T(8,128)} collective-permute-done((f32[2,256,128]{2,1,0:T(8,128)}, f32[2,256,128]{2,1,0:T(8,128)}, u32[]{:S(2)}, u32[]{:S(2)}) %collective-permute-start.2) | collective-permute-done | bytes 262176 | tf_op jit(solution)/shard_map/ppermute | solution.py:200
  25.6 4.8 %collective-permute-start.3 = (f32[2,256,128]{2,1,0:T(8,128)}, f32[2,256,128]{2,1,0:T(8,128)S(1)}, u32[]{:S(2)}, u32[]{:S(2)}) collective-permute-start(f32[2,256,128]{2,1,0:T(8,128)} %get-tuple-element.81), channel_id=1, source_target_pairs={{0,4},{4,0},{8,12},{12,8},{1,5},{5,1},{9,13},{13,9},{2,6},{6,2},{1... | collective-permute-start | bytes 786440 | tf_op jit(solution)/shard_map/ppermute | solution.py:200
  37.0 5.0 %collective-permute-start.5 = (f32[2,256,128]{2,1,0:T(8,128)S(1)}, f32[2,256,128]{2,1,0:T(8,128)S(1)}, u32[]{:S(2)}, u32[]{:S(2)}) collective-permute-start(f32[2,256,128]{2,1,0:T(8,128)S(1)} %select_select_fusion.31), channel_id=1, source_target_pairs={{0,4},{4,0},{8,12},{12,8},{1,5},{5,1},{9,13},{13,9},{2,6},{6,2},{1... | collective-permute-start | bytes 786440 | tf_op jit(solution)/shard_map/ppermute | solution.py:200
  44.2 5.4 %collective-permute-start.13 = (f32[2,256,128]{2,1,0:T(8,128)S(1)}, f32[2,256,128]{2,1,0:T(8,128)S(1)}, u32[]{:S(2)}, u32[]{:S(2)}) collective-permute-start(f32[2,256,128]{2,1,0:T(8,128)S(1)} %select_select_fusion.28), channel_id=1, source_target_pairs={{0,4},{4,0},{8,12},{12,8},{1,5},{5,1},{9,13},{13,9},{2,6},{6,2},{1... | collective-permute-start | bytes 786440 | tf_op jit(solution)/shard_map/ppermute | solution.py:200
  51.8 5.0 %collective-permute-done.13 = f32[2,256,128]{2,1,0:T(8,128)S(1)} collective-permute-done((f32[2,256,128]{2,1,0:T(8,128)S(1)}, f32[2,256,128]{2,1,0:T(8,128)S(1)}, u32[]{:S(2)}, u32[]{:S(2)}) %collective-permute-start.13) | collective-permute-done | bytes 262176 | tf_op jit(solution)/shard_map/ppermute | solution.py:200
  59.7 2.7 %collective-permute-done.7 = f32[2,256,128]{2,1,0:T(8,128)S(1)} collective-permute-done((f32[2,256,128]{2,1,0:T(8,128)S(1)}, f32[2,256,128]{2,1,0:T(8,128)S(1)}, u32[]{:S(2)}, u32[]{:S(2)}) %collective-permute-start.7) | collective-permute-done | bytes 262176 | tf_op jit(solution)/shard_map/ppermute | solution.py:200
  64.6 3.5 %collective-permute-done.15 = f32[2,256,128]{2,1,0:T(8,128)S(1)} collective-permute-done((f32[2,256,128]{2,1,0:T(8,128)S(1)}, f32[2,256,128]{2,1,0:T(8,128)S(1)}, u32[]{:S(2)}, u32[]{:S(2)}) %collective-permute-start.15) | collective-permute-done | bytes 262176 | tf_op jit(solution)/shard_map/ppermute | solution.py:200
  72.7 2.8 %collective-permute-done.17 = f32[2,256,128]{2,1,0:T(8,128)S(1)} collective-permute-done((f32[2,256,128]{2,1,0:T(8,128)S(1)}, f32[2,256,128]{2,1,0:T(8,128)S(1)}, u32[]{:S(2)}, u32[]{:S(2)}) %collective-permute-start.17) | collective-permute-done | bytes 262176 | tf_op jit(solution)/shard_map/ppermute | solution.py:200
  89.5 12.9 %collective-permute-start.27 = (f32[2,256,128]{2,1,0:T(8,128)S(1)}, f32[2,256,128]{2,1,0:T(8,128)S(1)}, u32[]{:S(2)}, u32[]{:S(2)}) collective-permute-start(f32[2,256,128]{2,1,0:T(8,128)S(1)} %select_select_fusion.15), channel_id=1, source_target_pairs={{0,4},{4,0},{8,12},{12,8},{1,5},{5,1},{9,13},{13,9},{2,6},{6,2},{1... | collective-permute-start | bytes 786440 | tf_op jit(solution)/shard_map/ppermute | solution.py:200
  106.7 8.5 %fold.1 = (bf16[1024,1024]{1,0:T(8,128)(2,1)S(1)}, bf16[1024,1024]{1,0:T(8,128)(2,1)S(1)}) custom-call(s32[18]{0:T(128)S(1)} %pad_add_fusion.numbers, f32[2,2,512,256]{3,2,1,0:T(8,128)S(1)} %broadcast_select_fusion.own_ref, f32[2,2,512,256]{3,2,1,0:T(8,128)} %collective-permute-done.18.other_ref, f32[2,2,64,256]{3,2,1,0:T(8,128)S(1)} %tile.10.op_ref), custom_call_target="tpu_custom_call" | custom-call | flops 6442450944 | bytes 8388608 | tf_op jit(solution)/shard_map/fold/pallas_call | solution.py:76
  120.2 5.1 %block.4.refs_4_ = f32[2,1024,1024]{2,1,0:T(8,128)} custom-call(bf16[1024,1024]{1,0:T(8,128)(2,1)S(1)} %get-tuple-element.107.upper_ref, bf16[1024,1024]{1,0:T(8,128)(2,1)S(1)} %get-tuple-element.108.lower_ref, f32[2,256,128]{2,1,0:T(8,128)S(1)} %get-tuple-element.187.refs_0_, f32[2,256,128]{2,1,0:T(8,128)S(1)} %get-tuple-element.184.refs_1_, ...), custom_call_target="tpu_custom_call" | custom-call | flops 3221225472 | bytes 6291456 | tf_op jit(solution)/shard_map/block/pallas_call | solution.py:143
  126.0 3.3 %collective-permute-done.22 = f32[2,256,128]{2,1,0:T(8,128)S(1)} collective-permute-done((f32[2,256,128]{2,1,0:T(8,128)S(1)}, f32[2,256,128]{2,1,0:T(8,128)S(1)}, u32[]{:S(2)}, u32[]{:S(2)}) %collective-permute-start.22) | collective-permute-done | bytes 262176 | tf_op jit(solution)/shard_map/ppermute | solution.py:200
  129.6 5.3 %collective-permute-start.33 = (f32[2,256,128]{2,1,0:T(8,128)S(1)}, f32[2,256,128]{2,1,0:T(8,128)S(1)}, u32[]{:S(2)}, u32[]{:S(2)}) collective-permute-start(f32[2,256,128]{2,1,0:T(8,128)S(1)} %select_select_fusion.8), channel_id=1, source_target_pairs={{0,4},{4,0},{8,12},{12,8},{1,5},{5,1},{9,13},{13,9},{2,6},{6,2},{1... | collective-permute-start | bytes 786440 | tf_op jit(solution)/shard_map/ppermute | solution.py:200
  136.4 5.1 %block.5.refs_4_ = f32[2,1024,1024]{2,1,0:T(8,128)} custom-call(bf16[1024,1024]{1,0:T(8,128)(2,1)S(1)} %get-tuple-element.107.upper_ref, bf16[1024,1024]{1,0:T(8,128)(2,1)S(1)} %get-tuple-element.108.lower_ref, f32[2,256,128]{2,1,0:T(8,128)S(1)} %get-tuple-element.181.refs_0_, ...), custom_call_target="tpu_custom_call", output_to_operand_aliasing={{}: (6, {})} | custom-call | flops 3221225472 | bytes 6291456 | tf_op jit(solution)/shard_map/block/pallas_call | solution.py:143
  141.5 3.3 %collective-permute-done.24 = f32[2,256,128]{2,1,0:T(8,128)S(1)} collective-permute-done((f32[2,256,128]{2,1,0:T(8,128)S(1)}, f32[2,256,128]{2,1,0:T(8,128)S(1)}, u32[]{:S(2)}, u32[]{:S(2)}) %collective-permute-start.24) | collective-permute-done | bytes 262176 | tf_op jit(solution)/shard_map/ppermute | solution.py:200
  144.8 3.2 %collective-permute-start.29 = (f32[2,256,128]{2,1,0:T(8,128)S(1)}, f32[2,256,128]{2,1,0:T(8,128)S(1)}, u32[]{:S(2)}, u32[]{:S(2)}) collective-permute-start(f32[2,256,128]{2,1,0:T(8,128)S(1)} %select_select_fusion.13), channel_id=1, source_target_pairs={{0,4},{4,0},{8,12},{12,8},{1,5},{5,1},{9,13},{13,9},{2,6},{6,2},{1... | collective-permute-start | bytes 786440 | tf_op jit(solution)/shard_map/ppermute | solution.py:200
  149.0 3.1 %collective-permute-start.36 = (f32[2,256,128]{2,1,0:T(8,128)S(1)}, f32[2,256,128]{2,1,0:T(8,128)S(1)}, u32[]{:S(2)}, u32[]{:S(2)}) collective-permute-start(f32[2,256,128]{2,1,0:T(8,128)S(1)} %select_select_fusion.3), channel_id=1, source_target_pairs={{0,4},{4,0},{8,12},{12,8},{1,5},{5,1},{9,13},{13,9},{2,6},{6,2},{1... | collective-permute-start | bytes 786440 | tf_op jit(solution)/shard_map/ppermute | solution.py:200
  152.7 5.1 %block.6.refs_4_ = f32[2,1024,1024]{2,1,0:T(8,128)} custom-call(bf16[1024,1024]{1,0:T(8,128)(2,1)S(1)} %get-tuple-element.107.upper_ref, bf16[1024,1024]{1,0:T(8,128)(2,1)S(1)} %get-tuple-element.108.lower_ref, f32[2,256,128]{2,1,0:T(8,128)S(1)} %get-tuple-element.179.refs_0_, ...), custom_call_target="tpu_custom_call", output_to_operand_aliasing={{}: (6, {})} | custom-call | flops 3221225472 | bytes 6291456 | tf_op jit(solution)/shard_map/block/pallas_call | solution.py:143
  161.8 4.2 %collective-permute-done.35 = f32[2,256,128]{2,1,0:T(8,128)S(1)} collective-permute-done((f32[2,256,128]{2,1,0:T(8,128)S(1)}, f32[2,256,128]{2,1,0:T(8,128)S(1)}, u32[]{:S(2)}, u32[]{:S(2)}) %collective-permute-start.35) | collective-permute-done | bytes 262176 | tf_op jit(solution)/shard_map/ppermute | solution.py:200
  166.0 2.8 %collective-permute-done.38 = f32[2,256,128]{2,1,0:T(8,128)S(1)} collective-permute-done((f32[2,256,128]{2,1,0:T(8,128)S(1)}, f32[2,256,128]{2,1,0:T(8,128)S(1)}, u32[]{:S(2)}, u32[]{:S(2)}) %collective-permute-start.38) | collective-permute-done | bytes 262176 | tf_op jit(solution)/shard_map/ppermute | solution.py:200
  168.9 5.1 %block.7 = f32[2,1024,1024]{2,1,0:T(8,128)} custom-call(bf16[1024,1024]{1,0:T(8,128)(2,1)S(1)} %get-tuple-element.107.upper_ref, bf16[1024,1024]{1,0:T(8,128)(2,1)S(1)} %get-tuple-element.108.lower_ref, f32[2,256,128]{2,1,0:T(8,128)S(1)} %select_select_fusion.6.refs_0_, ...), custom_call_target="tpu_custom_call", output_to_operand_aliasing={{}: (6, {})} | custom-call | flops 3221225472 | bytes 6291456 | tf_op jit(solution)/shard_map/block/pallas_call | solution.py:143
  (208 shorter events, 58.4 us)
Async XLA Ops:
  13.8 10.1 %collective-permute-start.2 = (f32[2,256,128]{2,1,0:T(8,128)}, f32[2,256,128]{2,1,0:T(8,128)}, u32[]{:S(2)}, u32[]{:S(2)}) collective-permute-start(f32[2,256,128]{2,1,0:T(8,128)} %get-tuple-element.80), channel_id=1, source_target_pairs={{0,4},{4,0},{8,12},{12,8},{1,5},{5,1},{9,13},{13,9},{2,6},{6,2},{1... | collective-permute-start | bytes 786440 | tf_op jit(solution)/shard_map/ppermute | solution.py:200
  16.5 16.2 %collective-permute-start.10 = (f32[2,256,128]{2,1,0:T(8,128)}, f32[2,256,128]{2,1,0:T(8,128)}, u32[]{:S(2)}, u32[]{:S(2)}) collective-permute-start(f32[2,256,128]{2,1,0:T(8,128)} %get-tuple-element.95), channel_id=1, source_target_pairs={{0,4},{4,0},{8,12},{12,8},{1,5},{5,1},{9,13},{13,9},{2,6},{6,2},{1... | collective-permute-start | bytes 786440 | tf_op jit(solution)/shard_map/ppermute | solution.py:200
  24.9 11.2 %collective-permute-start.4 = (f32[2,256,128]{2,1,0:T(8,128)S(1)}, f32[2,256,128]{2,1,0:T(8,128)S(1)}, u32[]{:S(2)}, u32[]{:S(2)}) collective-permute-start(f32[2,256,128]{2,1,0:T(8,128)S(1)} %broadcast_select_fusion.16), channel_id=1, source_target_pairs={{4,8},{8,4},{5,9},{9,5},{6,10},{10,6},{7,11},{11,7},{20,24},{24,20... | collective-permute-start | bytes 786440 | tf_op jit(solution)/shard_map/ppermute | solution.py:199
  25.6 10.6 %collective-permute-start.3 = (f32[2,256,128]{2,1,0:T(8,128)}, f32[2,256,128]{2,1,0:T(8,128)S(1)}, u32[]{:S(2)}, u32[]{:S(2)}) collective-permute-start(f32[2,256,128]{2,1,0:T(8,128)} %get-tuple-element.81), channel_id=1, source_target_pairs={{0,4},{4,0},{8,12},{12,8},{1,5},{5,1},{9,13},{13,9},{2,6},{6,2},{1... | collective-permute-start | bytes 786440 | tf_op jit(solution)/shard_map/ppermute | solution.py:200
  31.1 46.6 %collective-permute-start.1 = (f32[2,2,512,256]{3,2,1,0:T(8,128)}, f32[2,2,512,256]{3,2,1,0:T(8,128)S(1)}, u32[]{:S(2)}, u32[]{:S(2)}) collective-permute-start(f32[2,2,512,256]{3,2,1,0:T(8,128)} %maximum_select_fusion), channel_id=1, source_target_pairs={{0,2},{2,0},{1,3},{3,1},{4,6},{6,4},{5,7},{7,5},{8,10},{10,8},{9,1... | collective-permute-start | bytes 6291464 | tf_op jit(solution)/shard_map/ppermute | solution.py:247
  36.2 13.3 %collective-permute-start.6 = (f32[2,256,128]{2,1,0:T(8,128)S(1)}, f32[2,256,128]{2,1,0:T(8,128)S(1)}, u32[]{:S(2)}, u32[]{:S(2)}) collective-permute-start(f32[2,256,128]{2,1,0:T(8,128)S(1)} %broadcast_select_fusion.15), channel_id=1, source_target_pairs={{4,8},{8,4},{5,9},{9,5},{6,10},{10,6},{7,11},{11,7},{20,24},{24,20... | collective-permute-start | bytes 786440 | tf_op jit(solution)/shard_map/ppermute | solution.py:199
  37.0 12.6 %collective-permute-start.5 = (f32[2,256,128]{2,1,0:T(8,128)S(1)}, f32[2,256,128]{2,1,0:T(8,128)S(1)}, u32[]{:S(2)}, u32[]{:S(2)}) collective-permute-start(f32[2,256,128]{2,1,0:T(8,128)S(1)} %select_select_fusion.31), channel_id=1, source_target_pairs={{0,4},{4,0},{8,12},{12,8},{1,5},{5,1},{9,13},{13,9},{2,6},{6,2},{1... | collective-permute-start | bytes 786440 | tf_op jit(solution)/shard_map/ppermute | solution.py:200
  44.2 12.6 %collective-permute-start.13 = (f32[2,256,128]{2,1,0:T(8,128)S(1)}, f32[2,256,128]{2,1,0:T(8,128)S(1)}, u32[]{:S(2)}, u32[]{:S(2)}) collective-permute-start(f32[2,256,128]{2,1,0:T(8,128)S(1)} %select_select_fusion.28), channel_id=1, source_target_pairs={{0,4},{4,0},{8,12},{12,8},{1,5},{5,1},{9,13},{13,9},{2,6},{6,2},{1... | collective-permute-start | bytes 786440 | tf_op jit(solution)/shard_map/ppermute | solution.py:200
  49.7 12.7 %collective-permute-start.7 = (f32[2,256,128]{2,1,0:T(8,128)S(1)}, f32[2,256,128]{2,1,0:T(8,128)S(1)}, u32[]{:S(2)}, u32[]{:S(2)}) collective-permute-start(f32[2,256,128]{2,1,0:T(8,128)S(1)} %select_select_fusion.30), channel_id=1, source_target_pairs={{0,4},{4,0},{8,12},{12,8},{1,5},{5,1},{9,13},{13,9},{2,6},{6,2},{1... | collective-permute-start | bytes 786440 | tf_op jit(solution)/shard_map/ppermute | solution.py:200
  51.1 11.3 %collective-permute-start.8 = (f32[2,256,128]{2,1,0:T(8,128)S(1)}, f32[2,256,128]{2,1,0:T(8,128)S(1)}, u32[]{:S(2)}, u32[]{:S(2)}) collective-permute-start(f32[2,256,128]{2,1,0:T(8,128)S(1)} %get-tuple-element.188), channel_id=1, source_target_pairs={{4,8},{8,4},{5,9},{9,5},{6,10},{10,6},{7,11},{11,7},{20,24},{24,20... | collective-permute-start | bytes 786440 | tf_op jit(solution)/shard_map/ppermute | solution.py:199
  56.8 11.2 %collective-permute-start.15 = (f32[2,256,128]{2,1,0:T(8,128)S(1)}, f32[2,256,128]{2,1,0:T(8,128)S(1)}, u32[]{:S(2)}, u32[]{:S(2)}) collective-permute-start(f32[2,256,128]{2,1,0:T(8,128)S(1)} %select_select_fusion.27), channel_id=1, source_target_pairs={{0,4},{4,0},{8,12},{12,8},{1,5},{5,1},{9,13},{13,9},{2,6},{6,2},{1... | collective-permute-start | bytes 786440 | tf_op jit(solution)/shard_map/ppermute | solution.py:200
  62.5 10.2 %collective-permute-start.9 = (f32[2,256,128]{2,1,0:T(8,128)S(1)}, f32[2,256,128]{2,1,0:T(8,128)S(1)}, u32[]{:S(2)}, u32[]{:S(2)}) collective-permute-start(f32[2,256,128]{2,1,0:T(8,128)S(1)} %select_select_fusion.29), channel_id=1, source_target_pairs={{0,4},{4,0},{8,12},{12,8},{1,5},{5,1},{9,13},{13,9},{2,6},{6,2},{1... | collective-permute-start | bytes 786440 | tf_op jit(solution)/shard_map/ppermute | solution.py:200
  79.9 26.8 %collective-permute-start.18 = (f32[2,2,512,256]{3,2,1,0:T(8,128)S(1)}, f32[2,2,512,256]{3,2,1,0:T(8,128)}, u32[]{:S(2)}, u32[]{:S(2)}) collective-permute-start(f32[2,2,512,256]{3,2,1,0:T(8,128)S(1)} %broadcast_select_fusion.own_ref), channel_id=1, source_target_pairs={{0,1},{1,0},{2,3},{3,2},{4,5},{5,4},{6,7},{7,6},{8,9},{9,8},{10,11... | collective-permute-start | bytes 6291464 | tf_op jit(solution)/shard_map/ppermute | solution.py:267
  87.7 27.5 %collective-permute-start.28 = (f32[2,256,128]{2,1,0:T(8,128)S(1)}, f32[2,256,128]{2,1,0:T(8,128)S(1)}, u32[]{:S(2)}, u32[]{:S(2)}) collective-permute-start(f32[2,256,128]{2,1,0:T(8,128)S(1)} %broadcast_select_fusion.4), channel_id=1, source_target_pairs={{4,8},{8,4},{5,9},{9,5},{6,10},{10,6},{7,11},{11,7},{20,24},{24,20... | collective-permute-start | bytes 786440 | tf_op jit(solution)/shard_map/ppermute | solution.py:199
  89.5 25.7 %collective-permute-start.27 = (f32[2,256,128]{2,1,0:T(8,128)S(1)}, f32[2,256,128]{2,1,0:T(8,128)S(1)}, u32[]{:S(2)}, u32[]{:S(2)}) collective-permute-start(f32[2,256,128]{2,1,0:T(8,128)S(1)} %select_select_fusion.15), channel_id=1, source_target_pairs={{0,4},{4,0},{8,12},{12,8},{1,5},{5,1},{9,13},{13,9},{2,6},{6,2},{1... | collective-permute-start | bytes 786440 | tf_op jit(solution)/shard_map/ppermute | solution.py:200
  103.4 12.1 %collective-permute-start.21 = (f32[2,256,128]{2,1,0:T(8,128)S(1)}, f32[2,256,128]{2,1,0:T(8,128)S(1)}, u32[]{:S(2)}, u32[]{:S(2)}) collective-permute-start(f32[2,256,128]{2,1,0:T(8,128)S(1)} %broadcast_select_fusion.12), channel_id=1, source_target_pairs={{4,8},{8,4},{5,9},{9,5},{6,10},{10,6},{7,11},{11,7},{20,24},{24,20... | collective-permute-start | bytes 786440 | tf_op jit(solution)/shard_map/ppermute | solution.py:199
  105.2 10.3 %collective-permute-start.20 = (f32[2,256,128]{2,1,0:T(8,128)S(1)}, f32[2,256,128]{2,1,0:T(8,128)S(1)}, u32[]{:S(2)}, u32[]{:S(2)}) collective-permute-start(f32[2,256,128]{2,1,0:T(8,128)S(1)} %select_select_fusion.25), channel_id=1, source_target_pairs={{0,4},{4,0},{8,12},{12,8},{1,5},{5,1},{9,13},{13,9},{2,6},{6,2},{1... | collective-permute-start | bytes 786440 | tf_op jit(solution)/shard_map/ppermute | solution.py:200
  118.2 11.2 %collective-permute-start.22 = (f32[2,256,128]{2,1,0:T(8,128)S(1)}, f32[2,256,128]{2,1,0:T(8,128)S(1)}, u32[]{:S(2)}, u32[]{:S(2)}) collective-permute-start(f32[2,256,128]{2,1,0:T(8,128)S(1)} %select_select_fusion.24), channel_id=1, source_target_pairs={{0,4},{4,0},{8,12},{12,8},{1,5},{5,1},{9,13},{13,9},{2,6},{6,2},{1... | collective-permute-start | bytes 786440 | tf_op jit(solution)/shard_map/ppermute | solution.py:200
  118.8 10.6 %collective-permute-start.23 = (f32[2,256,128]{2,1,0:T(8,128)S(1)}, f32[2,256,128]{2,1,0:T(8,128)S(1)}, u32[]{:S(2)}, u32[]{:S(2)}) collective-permute-start(f32[2,256,128]{2,1,0:T(8,128)S(1)} %get-tuple-element.183), channel_id=1, source_target_pairs={{4,8},{8,4},{5,9},{9,5},{6,10},{10,6},{7,11},{11,7},{20,24},{24,20... | collective-permute-start | bytes 786440 | tf_op jit(solution)/shard_map/ppermute | solution.py:199
  129.6 19.3 %collective-permute-start.33 = (f32[2,256,128]{2,1,0:T(8,128)S(1)}, f32[2,256,128]{2,1,0:T(8,128)S(1)}, u32[]{:S(2)}, u32[]{:S(2)}) collective-permute-start(f32[2,256,128]{2,1,0:T(8,128)S(1)} %select_select_fusion.8), channel_id=1, source_target_pairs={{0,4},{4,0},{8,12},{12,8},{1,5},{5,1},{9,13},{13,9},{2,6},{6,2},{1... | collective-permute-start | bytes 786440 | tf_op jit(solution)/shard_map/ppermute | solution.py:200
  134.9 9.9 %collective-permute-start.24 = (f32[2,256,128]{2,1,0:T(8,128)S(1)}, f32[2,256,128]{2,1,0:T(8,128)S(1)}, u32[]{:S(2)}, u32[]{:S(2)}) collective-permute-start(f32[2,256,128]{2,1,0:T(8,128)S(1)} %select_select_fusion.19), channel_id=1, source_target_pairs={{0,4},{4,0},{8,12},{12,8},{1,5},{5,1},{9,13},{13,9},{2,6},{6,2},{1... | collective-permute-start | bytes 786440 | tf_op jit(solution)/shard_map/ppermute | solution.py:200
  135.7 13.2 %collective-permute-start.34 = (f32[2,256,128]{2,1,0:T(8,128)S(1)}, f32[2,256,128]{2,1,0:T(8,128)S(1)}, u32[]{:S(2)}, u32[]{:S(2)}) collective-permute-start(f32[2,256,128]{2,1,0:T(8,128)S(1)} %get-tuple-element.171), channel_id=1, source_target_pairs={{4,8},{8,4},{5,9},{9,5},{6,10},{10,6},{7,11},{11,7},{20,24},{24,20... | collective-permute-start | bytes 786440 | tf_op jit(solution)/shard_map/ppermute | solution.py:199
  144.8 12.9 %collective-permute-start.29 = (f32[2,256,128]{2,1,0:T(8,128)S(1)}, f32[2,256,128]{2,1,0:T(8,128)S(1)}, u32[]{:S(2)}, u32[]{:S(2)}) collective-permute-start(f32[2,256,128]{2,1,0:T(8,128)S(1)} %select_select_fusion.13), channel_id=1, source_target_pairs={{0,4},{4,0},{8,12},{12,8},{1,5},{5,1},{9,13},{13,9},{2,6},{6,2},{1... | collective-permute-start | bytes 786440 | tf_op jit(solution)/shard_map/ppermute | solution.py:200
  149.0 11.0 %collective-permute-start.36 = (f32[2,256,128]{2,1,0:T(8,128)S(1)}, f32[2,256,128]{2,1,0:T(8,128)S(1)}, u32[]{:S(2)}, u32[]{:S(2)}) collective-permute-start(f32[2,256,128]{2,1,0:T(8,128)S(1)} %select_select_fusion.3), channel_id=1, source_target_pairs={{0,4},{4,0},{8,12},{12,8},{1,5},{5,1},{9,13},{13,9},{2,6},{6,2},{1... | collective-permute-start | bytes 786440 | tf_op jit(solution)/shard_map/ppermute | solution.py:200
  (65 other events, 689.4 us)

commit v2 on v1

--- a/solution.py
+++ b/solution.py
@@ -11,8 +11,8 @@
 LINE = 4
 PIECES = 8
 GROUP = 2
-MINE, COLUMNS, FOLD = 1, 5, 6
-BLOCKS = {7: (0,), 8: (2,), 9: (4,)}
+MINE, COLUMNS, FOLD = 1, 5, 7
+BLOCKS = {8: (0,), 9: (2, 4)}
 
 
 def split(value):
@@ -69,15 +69,15 @@
 
 def fold(numbers, own, other, ops):
     streams, _, rows, order = own.shape
-    tile = rows // 2
+    tile = rows
     shape = jax.ShapeDtypeStruct((2 * rows, streams * 2 * order), jnp.bfloat16)
     slab_spec = pl.BlockSpec((1, 2, tile, order), lambda k, h, i, numbers: (k, 0, i, 0))
-    out_spec = pl.BlockSpec((tile, 2 * order), lambda k, h, i, numbers: (2 * h + i, k))
+    out_spec = pl.BlockSpec((tile, 2 * order), lambda k, h, i, numbers: (h + i, k))
     return pl.pallas_call(
         fold_kernel,
         grid_spec=pltpu.PrefetchScalarGridSpec(
             num_scalar_prefetch=1,
-            grid=(streams, 2, 2),
+            grid=(streams, 2, 1),
             in_specs=[
                 slab_spec,
                 slab_spec,

time: 175 us -> 166 us (0.949)
  waiting for transfers between devices: 37 us -> 30 us
  Pallas kernels: 28.9 us -> 26.9 us
    ppermute x20, waiting for transfers between devices: 34.7 us -> 28.2 us  [step(): lax.ppermute(value, 'row', [(0, 1), (1, 0), (2, 3), (3, 2)])]
    pallas_call x1, Pallas kernels: 8.54 us -> 6.6 us  [fold(): pl.pallas_call(fold_kernel, grid_spec=pltpu.PrefetchScalarGridSpec(num_sc...]
    select_n x11 -> x12, other arithmetic: 5.82 us -> 5.16 us  [step(): jnp.where(self.holder, self.own[index - 1], self.outer[index - 1])]
  transfers between devices with their start and end apart: 39 -> 39, of which waited for: 13 -> 14; matrix products, arithmetic and copies ran while one was open for 11% -> 13% of each run, Pallas kernels for 14% -> 13%
where the time goes in v2:
time: 166 us
  starting transfers between devices  73.1 us (44%)
  waiting for transfers between devices  30 us (18%)
  Pallas kernels  26.9 us (16%)
  other arithmetic  16.6 us (10%)
  local copies, waits for them, and re-layouts  12.9 us (8%)
  between operations  6.14 us (4%)
    ppermute x20, starting transfers between devices, step(): lax.ppermute(value, 'row', [(0, 1), (1, 0), (2, 3), (3, 2)])  58.3 us
    ppermute x20, waiting for transfers between devices, step(): lax.ppermute(value, 'row', [(0, 1), (1, 0), (2, 3), (3, 2)])  28.2 us
    pallas_call x4, Pallas kernels, block(): pl.pallas_call(block_kernel, grid=(row_count // tile,), in_specs=specs, o...  20.3 us
    ppermute x16, starting transfers between devices, step(): self.inner.append(lax.ppermute(crossing, 'row', [(1, 2), (2, 1)]))  12.7 us
    pallas_call x1, Pallas kernels, fold(): pl.pallas_call(fold_kernel, grid_spec=pltpu.PrefetchScalarGridSpec(num_sc...  6.6 us
    select_n x12, other arithmetic, step(): jnp.where(self.holder, self.own[index - 1], self.outer[index - 1])  5.16 us
    slice x1, local copies, waits for them, and re-layouts, __init__(): lax.slice_in_dim(slab, p * self.width, (p + 1) * self.width, axis=2)  3.9 us
  transfers between devices with their start and end apart: 39, of which 14 were waited for; matrix products, arithmetic and copies ran while one was open for 13% of the time, Pallas kernels for 13%

profile of v2, /device:TPU:0, one launch (start us, length us, event | category | flops | bytes accessed | tf_op | source)
XLA Modules:
  0.0 165.7 jit_solution(2132957465090378685)
XLA Ops:
  5.3 2.7 %dynamic-slice_bitcast_fusion.3 = (f32[1,2,512,256]{3,2,1,0:T(8,128)S(1)}, f32[1,2,512,256]{3,2,1,0:T(8,128)S(1)}, f32[1,2,512,256]{3,2,1,0:T(8,128)S(1)}, f32[1,2,512,256]{3,2,1,0:T(8,128)S(1)}) fusion(f32[2,1024,1024]{2,1,0:T(8,128)} %param.5, s32[]{:T(128)S(6)} %select_n.494, s32[]{:T(128)S(6)} %select_n.496, s32[]{:T(128)S(6)} %select_n.499, s32[]{:T(128)S(6)} %select_n.498), kind=kLoop, calls=%fused_computation.5 | loop fusion | bytes 8388624 | tf_op jit(solution)/shard_map/stack | solution.py:232
  10.1 3.9 %constant_dynamic-slice_fusion.14 = (f32[2,256,128]{2,1,0:T(8,128)S(1)}, f32[2,256,128]{2,1,0:T(8,128)}, f32[2,256,128]{2,1,0:T(8,128)}, f32[2,256,128]{2,1,0:T(...) fusion(f32[2,1024,1024]{2,1,0:T(8,128)} %param.5, ...), kind=kLoop, calls=%fused_computation.69 | loop fusion | bytes 8388644 | tf_op jit(solution)/shard_map/slice | solution.py:180
  17.5 3.2 %maximum_select_fusion = f32[2,2,512,256]{3,2,1,0:T(8,128)} fusion(f32[2,2,512,256]{3,2,1,0:T(8,128)} %collective-permute-done, f32[1,2,512,256]{3,2,1,0:T(8,128)S(1)} %get-tuple-element.168, f32[1,2,512,256]{3,2,1,0:T(8,128)S(1)} %get-tuple-element.165, pred[2]{0:T(512)(128)(4,1)S(1)} %fusion), kind=kLoop, calls=%fused_computation | loop fusion | flops 1048576 | bytes 6291458 | tf_op jit(solution)/shard_map/jit(_where)/select_n | solution.py:246
  20.7 3.4 %collective-permute-done.2 = f32[2,256,128]{2,1,0:T(8,128)} collective-permute-done((f32[2,256,128]{2,1,0:T(8,128)}, f32[2,256,128]{2,1,0:T(8,128)}, u32[]{:S(2)}, u32[]{:S(2)}) %collective-permute-start.2) | collective-permute-done | bytes 262176 | tf_op jit(solution)/shard_map/ppermute | solution.py:200
  25.8 4.8 %collective-permute-start.3 = (f32[2,256,128]{2,1,0:T(8,128)}, f32[2,256,128]{2,1,0:T(8,128)S(1)}, u32[]{:S(2)}, u32[]{:S(2)}) collective-permute-start(f32[2,256,128]{2,1,0:T(8,128)} %get-tuple-element.81), channel_id=1, source_target_pairs={{0,4},{4,0},{8,12},{12,8},{1,5},{5,1},{9,13},{13,9},{2,6},{6,2},{1... | collective-permute-start | bytes 786440 | tf_op jit(solution)/shard_map/ppermute | solution.py:200
  37.3 3.5 %collective-permute-start.5 = (f32[2,256,128]{2,1,0:T(8,128)S(1)}, f32[2,256,128]{2,1,0:T(8,128)S(1)}, u32[]{:S(2)}, u32[]{:S(2)}) collective-permute-start(f32[2,256,128]{2,1,0:T(8,128)S(1)} %select_select_fusion.31), channel_id=1, source_target_pairs={{0,4},{4,0},{8,12},{12,8},{1,5},{5,1},{9,13},{13,9},{2,6},{6,2},{1... | collective-permute-start | bytes 786440 | tf_op jit(solution)/shard_map/ppermute | solution.py:200
  40.7 3.4 %collective-permute-done.11 = f32[2,256,128]{2,1,0:T(8,128)S(1)} collective-permute-done((f32[2,256,128]{2,1,0:T(8,128)}, f32[2,256,128]{2,1,0:T(8,128)S(1)}, u32[]{:S(2)}, u32[]{:S(2)}) %collective-permute-start.11) | collective-permute-done | bytes 262176 | tf_op jit(solution)/shard_map/ppermute | solution.py:200
  44.9 3.7 %collective-permute-start.13 = (f32[2,256,128]{2,1,0:T(8,128)S(1)}, f32[2,256,128]{2,1,0:T(8,128)S(1)}, u32[]{:S(2)}, u32[]{:S(2)}) collective-permute-start(f32[2,256,128]{2,1,0:T(8,128)S(1)} %select_select_fusion.28), channel_id=1, source_target_pairs={{0,4},{4,0},{8,12},{12,8},{1,5},{5,1},{9,13},{13,9},{2,6},{6,2},{1... | collective-permute-start | bytes 786440 | tf_op jit(solution)/shard_map/ppermute | solution.py:200
  51.4 3.7 %collective-permute-start.7 = (f32[2,256,128]{2,1,0:T(8,128)S(1)}, f32[2,256,128]{2,1,0:T(8,128)S(1)}, u32[]{:S(2)}, u32[]{:S(2)}) collective-permute-start(f32[2,256,128]{2,1,0:T(8,128)S(1)} %select_select_fusion.30), channel_id=1, source_target_pairs={{0,4},{4,0},{8,12},{12,8},{1,5},{5,1},{9,13},{13,9},{2,6},{6,2},{1... | collective-permute-start | bytes 786440 | tf_op jit(solution)/shard_map/ppermute | solution.py:200
  56.7 4.3 %collective-permute-start.15 = (f32[2,256,128]{2,1,0:T(8,128)S(1)}, f32[2,256,128]{2,1,0:T(8,128)S(1)}, u32[]{:S(2)}, u32[]{:S(2)}) collective-permute-start(f32[2,256,128]{2,1,0:T(8,128)S(1)} %select_select_fusion.27), channel_id=1, source_target_pairs={{0,4},{4,0},{8,12},{12,8},{1,5},{5,1},{9,13},{13,9},{2,6},{6,2},{1... | collective-permute-start | bytes 786440 | tf_op jit(solution)/shard_map/ppermute | solution.py:200
  73.4 2.8 %collective-permute-done.17 = f32[2,256,128]{2,1,0:T(8,128)S(1)} collective-permute-done((f32[2,256,128]{2,1,0:T(8,128)S(1)}, f32[2,256,128]{2,1,0:T(8,128)S(1)}, u32[]{:S(2)}, u32[]{:S(2)}) %collective-permute-start.17) | collective-permute-done | bytes 262176 | tf_op jit(solution)/shard_map/ppermute | solution.py:200
  85.7 3.1 %collective-permute-start.29 = (f32[2,256,128]{2,1,0:T(8,128)S(1)}, f32[2,256,128]{2,1,0:T(8,128)S(1)}, u32[]{:S(2)}, u32[]{:S(2)}) collective-permute-start(f32[2,256,128]{2,1,0:T(8,128)S(1)} %select_select_fusion.15), channel_id=1, source_target_pairs={{0,4},{4,0},{8,12},{12,8},{1,5},{5,1},{9,13},{13,9},{2,6},{6,2},{1... | collective-permute-start | bytes 786440 | tf_op jit(solution)/shard_map/ppermute | solution.py:200
  96.7 4.4 %collective-permute-start.31 = (f32[2,256,128]{2,1,0:T(8,128)S(1)}, f32[2,256,128]{2,1,0:T(8,128)S(1)}, u32[]{:S(2)}, u32[]{:S(2)}) collective-permute-start(f32[2,256,128]{2,1,0:T(8,128)S(1)} %select_select_fusion.14), channel_id=1, source_target_pairs={{0,4},{4,0},{8,12},{12,8},{1,5},{5,1},{9,13},{13,9},{2,6},{6,2},{1... | collective-permute-start | bytes 786440 | tf_op jit(solution)/shard_map/ppermute | solution.py:200
  102.3 4.4 %collective-permute-start.22 = (f32[2,256,128]{2,1,0:T(8,128)S(1)}, f32[2,256,128]{2,1,0:T(8,128)S(1)}, u32[]{:S(2)}, u32[]{:S(2)}) collective-permute-start(f32[2,256,128]{2,1,0:T(8,128)S(1)} %select_select_fusion.24), channel_id=1, source_target_pairs={{0,4},{4,0},{8,12},{12,8},{1,5},{5,1},{9,13},{13,9},{2,6},{6,2},{1... | collective-permute-start | bytes 786440 | tf_op jit(solution)/shard_map/ppermute | solution.py:200
  106.8 6.6 %fold.1 = (bf16[1024,1024]{1,0:T(8,128)(2,1)S(1)}, bf16[1024,1024]{1,0:T(8,128)(2,1)S(1)}) custom-call(s32[18]{0:T(128)S(1)} %pad_add_fusion.numbers, f32[2,2,512,256]{3,2,1,0:T(8,128)S(1)} %broadcast_select_fusion.own_ref, f32[2,2,512,256]{3,2,1,0:T(8,128)} %collective-permute-done.18.other_ref, f32[2,2,64,256]{3,2,1,0:T(8,128)S(1)} %tile.10.op_ref), custom_call_target="tpu_custom_call" | custom-call | flops 6442450944 | bytes 8388608 | tf_op jit(solution)/shard_map/fold/pallas_call | solution.py:76
  118.5 5.1 %block.4.refs_4_ = f32[2,1024,1024]{2,1,0:T(8,128)} custom-call(bf16[1024,1024]{1,0:T(8,128)(2,1)S(1)} %get-tuple-element.107.upper_ref, bf16[1024,1024]{1,0:T(8,128)(2,1)S(1)} %get-tuple-element.108.lower_ref, f32[2,256,128]{2,1,0:T(8,128)S(1)} %get-tuple-element.182.refs_0_, f32[2,256,128]{2,1,0:T(8,128)S(1)} %get-tuple-element.185.refs_1_, ...), custom_call_target="tpu_custom_call" | custom-call | flops 3221225472 | bytes 6291456 | tf_op jit(solution)/shard_map/block/pallas_call | solution.py:143
  124.2 2.7 %collective-permute-done.24 = f32[2,256,128]{2,1,0:T(8,128)S(1)} collective-permute-done((f32[2,256,128]{2,1,0:T(8,128)S(1)}, f32[2,256,128]{2,1,0:T(8,128)S(1)}, u32[]{:S(2)}, u32[]{:S(2)}) %collective-permute-start.24) | collective-permute-done | bytes 262176 | tf_op jit(solution)/shard_map/ppermute | solution.py:200
  127.1 6.3 %collective-permute-start.36 = (f32[2,256,128]{2,1,0:T(8,128)S(1)}, f32[2,256,128]{2,1,0:T(8,128)S(1)}, u32[]{:S(2)}, u32[]{:S(2)}) collective-permute-start(f32[2,256,128]{2,1,0:T(8,128)S(1)} %select_select_fusion.3), channel_id=1, source_target_pairs={{0,4},{4,0},{8,12},{12,8},{1,5},{5,1},{9,13},{13,9},{2,6},{6,2},{1... | collective-permute-start | bytes 786440 | tf_op jit(solution)/shard_map/ppermute | solution.py:200
  135.1 5.1 %block.5.refs_4_ = f32[2,1024,1024]{2,1,0:T(8,128)} custom-call(bf16[1024,1024]{1,0:T(8,128)(2,1)S(1)} %get-tuple-element.107.upper_ref, bf16[1024,1024]{1,0:T(8,128)(2,1)S(1)} %get-tuple-element.108.lower_ref, f32[2,256,128]{2,1,0:T(8,128)S(1)} %get-tuple-element.179.refs_0_, ...), custom_call_target="tpu_custom_call", output_to_operand_aliasing={{}: (6, {})} | custom-call | flops 3221225472 | bytes 6291456 | tf_op jit(solution)/shard_map/block/pallas_call | solution.py:143
  140.2 5.1 %block.6.refs_4_ = f32[2,1024,1024]{2,1,0:T(8,128)} custom-call(bf16[1024,1024]{1,0:T(8,128)(2,1)S(1)} %get-tuple-element.107.upper_ref, bf16[1024,1024]{1,0:T(8,128)(2,1)S(1)} %get-tuple-element.108.lower_ref, f32[2,256,128]{2,1,0:T(8,128)S(1)} %get-tuple-element.180.refs_0_, ...), custom_call_target="tpu_custom_call", output_to_operand_aliasing={{}: (6, {})} | custom-call | flops 3221225472 | bytes 6291456 | tf_op jit(solution)/shard_map/block/pallas_call | solution.py:143
  145.3 6.6 %collective-permute-start.35 = (f32[2,256,128]{2,1,0:T(8,128)S(1)}, f32[2,256,128]{2,1,0:T(8,128)S(1)}, u32[]{:S(2)}, u32[]{:S(2)}) collective-permute-start(f32[2,256,128]{2,1,0:T(8,128)S(1)} %select_select_fusion.5), channel_id=1, source_target_pairs={{0,4},{4,0},{8,12},{12,8},{1,5},{5,1},{9,13},{13,9},{2,6},{6,2},{1... | collective-permute-start | bytes 786440 | tf_op jit(solution)/shard_map/ppermute | solution.py:200
  152.1 5.6 %collective-permute-done.35 = f32[2,256,128]{2,1,0:T(8,128)S(1)} collective-permute-done((f32[2,256,128]{2,1,0:T(8,128)S(1)}, f32[2,256,128]{2,1,0:T(8,128)S(1)}, u32[]{:S(2)}, u32[]{:S(2)}) %collective-permute-start.35) | collective-permute-done | bytes 262176 | tf_op jit(solution)/shard_map/ppermute | solution.py:200
  157.8 2.7 %collective-permute-done.38 = f32[2,256,128]{2,1,0:T(8,128)S(1)} collective-permute-done((f32[2,256,128]{2,1,0:T(8,128)S(1)}, f32[2,256,128]{2,1,0:T(8,128)S(1)}, u32[]{:S(2)}, u32[]{:S(2)}) %collective-permute-start.38) | collective-permute-done | bytes 262176 | tf_op jit(solution)/shard_map/ppermute | solution.py:200
  160.6 5.1 %block.7 = f32[2,1024,1024]{2,1,0:T(8,128)} custom-call(bf16[1024,1024]{1,0:T(8,128)(2,1)S(1)} %get-tuple-element.107.upper_ref, bf16[1024,1024]{1,0:T(8,128)(2,1)S(1)} %get-tuple-element.108.lower_ref, f32[2,256,128]{2,1,0:T(8,128)S(1)} %select_select_fusion.6.refs_0_, ...), custom_call_target="tpu_custom_call", output_to_operand_aliasing={{}: (6, {})} | custom-call | flops 3221225472 | bytes 6291456 | tf_op jit(solution)/shard_map/block/pallas_call | solution.py:143
  (202 shorter events, 57.5 us)
Async XLA Ops:
  16.7 16.3 %collective-permute-start.10 = (f32[2,256,128]{2,1,0:T(8,128)}, f32[2,256,128]{2,1,0:T(8,128)}, u32[]{:S(2)}, u32[]{:S(2)}) collective-permute-start(f32[2,256,128]{2,1,0:T(8,128)} %get-tuple-element.95), channel_id=1, source_target_pairs={{0,4},{4,0},{8,12},{12,8},{1,5},{5,1},{9,13},{13,9},{2,6},{6,2},{1... | collective-permute-start | bytes 786440 | tf_op jit(solution)/shard_map/ppermute | solution.py:200
  25.2 11.3 %collective-permute-start.4 = (f32[2,256,128]{2,1,0:T(8,128)S(1)}, f32[2,256,128]{2,1,0:T(8,128)S(1)}, u32[]{:S(2)}, u32[]{:S(2)}) collective-permute-start(f32[2,256,128]{2,1,0:T(8,128)S(1)} %broadcast_select_fusion.16), channel_id=1, source_target_pairs={{4,8},{8,4},{5,9},{9,5},{6,10},{10,6},{7,11},{11,7},{20,24},{24,20... | collective-permute-start | bytes 786440 | tf_op jit(solution)/shard_map/ppermute | solution.py:199
  25.8 10.6 %collective-permute-start.3 = (f32[2,256,128]{2,1,0:T(8,128)}, f32[2,256,128]{2,1,0:T(8,128)S(1)}, u32[]{:S(2)}, u32[]{:S(2)}) collective-permute-start(f32[2,256,128]{2,1,0:T(8,128)} %get-tuple-element.81), channel_id=1, source_target_pairs={{0,4},{4,0},{8,12},{12,8},{1,5},{5,1},{9,13},{13,9},{2,6},{6,2},{1... | collective-permute-start | bytes 786440 | tf_op jit(solution)/shard_map/ppermute | solution.py:200
  31.4 46.6 %collective-permute-start.1 = (f32[2,2,512,256]{3,2,1,0:T(8,128)}, f32[2,2,512,256]{3,2,1,0:T(8,128)S(1)}, u32[]{:S(2)}, u32[]{:S(2)}) collective-permute-start(f32[2,2,512,256]{3,2,1,0:T(8,128)} %maximum_select_fusion), channel_id=1, source_target_pairs={{0,2},{2,0},{1,3},{3,1},{4,6},{6,4},{5,7},{7,5},{8,10},{10,8},{9,1... | collective-permute-start | bytes 6291464 | tf_op jit(solution)/shard_map/ppermute | solution.py:247
  36.5 12.1 %collective-permute-start.6 = (f32[2,256,128]{2,1,0:T(8,128)S(1)}, f32[2,256,128]{2,1,0:T(8,128)S(1)}, u32[]{:S(2)}, u32[]{:S(2)}) collective-permute-start(f32[2,256,128]{2,1,0:T(8,128)S(1)} %broadcast_select_fusion.15), channel_id=1, source_target_pairs={{4,8},{8,4},{5,9},{9,5},{6,10},{10,6},{7,11},{11,7},{20,24},{24,20... | collective-permute-start | bytes 786440 | tf_op jit(solution)/shard_map/ppermute | solution.py:199
  37.3 12.5 %collective-permute-start.5 = (f32[2,256,128]{2,1,0:T(8,128)S(1)}, f32[2,256,128]{2,1,0:T(8,128)S(1)}, u32[]{:S(2)}, u32[]{:S(2)}) collective-permute-start(f32[2,256,128]{2,1,0:T(8,128)S(1)} %select_select_fusion.31), channel_id=1, source_target_pairs={{0,4},{4,0},{8,12},{12,8},{1,5},{5,1},{9,13},{13,9},{2,6},{6,2},{1... | collective-permute-start | bytes 786440 | tf_op jit(solution)/shard_map/ppermute | solution.py:200
  44.1 10.9 %collective-permute-start.14 = (f32[2,256,128]{2,1,0:T(8,128)S(1)}, f32[2,256,128]{2,1,0:T(8,128)S(1)}, u32[]{:S(2)}, u32[]{:S(2)}) collective-permute-start(f32[2,256,128]{2,1,0:T(8,128)S(1)} %broadcast_select_fusion.7), channel_id=1, source_target_pairs={{4,8},{8,4},{5,9},{9,5},{6,10},{10,6},{7,11},{11,7},{20,24},{24,20... | collective-permute-start | bytes 786440 | tf_op jit(solution)/shard_map/ppermute | solution.py:199
  55.8 10.6 %collective-permute-start.16 = (f32[2,256,128]{2,1,0:T(8,128)S(1)}, f32[2,256,128]{2,1,0:T(8,128)S(1)}, u32[]{:S(2)}, u32[]{:S(2)}) collective-permute-start(f32[2,256,128]{2,1,0:T(8,128)S(1)} %broadcast_select_fusion.6), channel_id=1, source_target_pairs={{4,8},{8,4},{5,9},{9,5},{6,10},{10,6},{7,11},{11,7},{20,24},{24,20... | collective-permute-start | bytes 786440 | tf_op jit(solution)/shard_map/ppermute | solution.py:199
  56.7 11.5 %collective-permute-start.15 = (f32[2,256,128]{2,1,0:T(8,128)S(1)}, f32[2,256,128]{2,1,0:T(8,128)S(1)}, u32[]{:S(2)}, u32[]{:S(2)}) collective-permute-start(f32[2,256,128]{2,1,0:T(8,128)S(1)} %select_select_fusion.27), channel_id=1, source_target_pairs={{0,4},{4,0},{8,12},{12,8},{1,5},{5,1},{9,13},{13,9},{2,6},{6,2},{1... | collective-permute-start | bytes 786440 | tf_op jit(solution)/shard_map/ppermute | solution.py:200
  62.0 11.4 %collective-permute-start.9 = (f32[2,256,128]{2,1,0:T(8,128)S(1)}, f32[2,256,128]{2,1,0:T(8,128)S(1)}, u32[]{:S(2)}, u32[]{:S(2)}) collective-permute-start(f32[2,256,128]{2,1,0:T(8,128)S(1)} %select_select_fusion.29), channel_id=1, source_target_pairs={{0,4},{4,0},{8,12},{12,8},{1,5},{5,1},{9,13},{13,9},{2,6},{6,2},{1... | collective-permute-start | bytes 786440 | tf_op jit(solution)/shard_map/ppermute | solution.py:200
  65.1 17.8 %collective-permute-start.19 = (f32[2,256,128]{2,1,0:T(8,128)}, f32[2,256,128]{2,1,0:T(8,128)}, u32[]{:S(2)}, u32[]{:S(2)}) collective-permute-start(f32[2,256,128]{2,1,0:T(8,128)} %get-tuple-element.186), channel_id=1, source_target_pairs={{4,8},{8,4},{5,9},{9,5},{6,10},{10,6},{7,11},{11,7},{20,24},{24,20... | collective-permute-start | bytes 786440 | tf_op jit(solution)/shard_map/ppermute | solution.py:199
  71.1 11.7 %collective-permute-start.28 = (f32[2,256,128]{2,1,0:T(8,128)}, f32[2,256,128]{2,1,0:T(8,128)}, u32[]{:S(2)}, u32[]{:S(2)}) collective-permute-start(f32[2,256,128]{2,1,0:T(8,128)} %get-tuple-element.183), channel_id=1, source_target_pairs={{4,8},{8,4},{5,9},{9,5},{6,10},{10,6},{7,11},{11,7},{20,24},{24,20... | collective-permute-start | bytes 786440 | tf_op jit(solution)/shard_map/ppermute | solution.py:199
  80.2 26.6 %collective-permute-start.18 = (f32[2,2,512,256]{3,2,1,0:T(8,128)S(1)}, f32[2,2,512,256]{3,2,1,0:T(8,128)}, u32[]{:S(2)}, u32[]{:S(2)}) collective-permute-start(f32[2,2,512,256]{3,2,1,0:T(8,128)S(1)} %broadcast_select_fusion.own_ref), channel_id=1, source_target_pairs={{0,1},{1,0},{2,3},{3,2},{4,5},{5,4},{6,7},{7,6},{8,9},{9,8},{10,11... | collective-permute-start | bytes 6291464 | tf_op jit(solution)/shard_map/ppermute | solution.py:267
  89.8 11.4 %collective-permute-start.21 = (f32[2,256,128]{2,1,0:T(8,128)S(1)}, f32[2,256,128]{2,1,0:T(8,128)S(1)}, u32[]{:S(2)}, u32[]{:S(2)}) collective-permute-start(f32[2,256,128]{2,1,0:T(8,128)S(1)} %broadcast_select_fusion.12), channel_id=1, source_target_pairs={{4,8},{8,4},{5,9},{9,5},{6,10},{10,6},{7,11},{11,7},{20,24},{24,20... | collective-permute-start | bytes 786440 | tf_op jit(solution)/shard_map/ppermute | solution.py:199
  95.9 17.5 %collective-permute-start.32 = (f32[2,256,128]{2,1,0:T(8,128)S(1)}, f32[2,256,128]{2,1,0:T(8,128)S(1)}, u32[]{:S(2)}, u32[]{:S(2)}) collective-permute-start(f32[2,256,128]{2,1,0:T(8,128)S(1)} %broadcast_select_fusion.3), channel_id=1, source_target_pairs={{4,8},{8,4},{5,9},{9,5},{6,10},{10,6},{7,11},{11,7},{20,24},{24,20... | collective-permute-start | bytes 786440 | tf_op jit(solution)/shard_map/ppermute | solution.py:199
  96.7 16.8 %collective-permute-start.31 = (f32[2,256,128]{2,1,0:T(8,128)S(1)}, f32[2,256,128]{2,1,0:T(8,128)S(1)}, u32[]{:S(2)}, u32[]{:S(2)}) collective-permute-start(f32[2,256,128]{2,1,0:T(8,128)S(1)} %select_select_fusion.14), channel_id=1, source_target_pairs={{0,4},{4,0},{8,12},{12,8},{1,5},{5,1},{9,13},{13,9},{2,6},{6,2},{1... | collective-permute-start | bytes 786440 | tf_op jit(solution)/shard_map/ppermute | solution.py:200
  101.5 12.2 %collective-permute-start.23 = (f32[2,256,128]{2,1,0:T(8,128)S(1)}, f32[2,256,128]{2,1,0:T(8,128)S(1)}, u32[]{:S(2)}, u32[]{:S(2)}) collective-permute-start(f32[2,256,128]{2,1,0:T(8,128)S(1)} %broadcast_select_fusion.11), channel_id=1, source_target_pairs={{4,8},{8,4},{5,9},{9,5},{6,10},{10,6},{7,11},{11,7},{20,24},{24,20... | collective-permute-start | bytes 786440 | tf_op jit(solution)/shard_map/ppermute | solution.py:199
  102.3 11.4 %collective-permute-start.22 = (f32[2,256,128]{2,1,0:T(8,128)S(1)}, f32[2,256,128]{2,1,0:T(8,128)S(1)}, u32[]{:S(2)}, u32[]{:S(2)}) collective-permute-start(f32[2,256,128]{2,1,0:T(8,128)S(1)} %select_select_fusion.24), channel_id=1, source_target_pairs={{0,4},{4,0},{8,12},{12,8},{1,5},{5,1},{9,13},{13,9},{2,6},{6,2},{1... | collective-permute-start | bytes 786440 | tf_op jit(solution)/shard_map/ppermute | solution.py:200
  115.0 11.9 %collective-permute-start.24 = (f32[2,256,128]{2,1,0:T(8,128)S(1)}, f32[2,256,128]{2,1,0:T(8,128)S(1)}, u32[]{:S(2)}, u32[]{:S(2)}) collective-permute-start(f32[2,256,128]{2,1,0:T(8,128)S(1)} %select_select_fusion.23), channel_id=1, source_target_pairs={{0,4},{4,0},{8,12},{12,8},{1,5},{5,1},{9,13},{13,9},{2,6},{6,2},{1... | collective-permute-start | bytes 786440 | tf_op jit(solution)/shard_map/ppermute | solution.py:200
  127.1 24.8 %collective-permute-start.36 = (f32[2,256,128]{2,1,0:T(8,128)S(1)}, f32[2,256,128]{2,1,0:T(8,128)S(1)}, u32[]{:S(2)}, u32[]{:S(2)}) collective-permute-start(f32[2,256,128]{2,1,0:T(8,128)S(1)} %select_select_fusion.3), channel_id=1, source_target_pairs={{0,4},{4,0},{8,12},{12,8},{1,5},{5,1},{9,13},{13,9},{2,6},{6,2},{1... | collective-permute-start | bytes 786440 | tf_op jit(solution)/shard_map/ppermute | solution.py:200
  133.4 11.8 %collective-permute-start.26 = (f32[2,256,128]{2,1,0:T(8,128)S(1)}, f32[2,256,128]{2,1,0:T(8,128)S(1)}, u32[]{:S(2)}, u32[]{:S(2)}) collective-permute-start(f32[2,256,128]{2,1,0:T(8,128)S(1)} %select_select_fusion.18), channel_id=1, source_target_pairs={{0,4},{4,0},{8,12},{12,8},{1,5},{5,1},{9,13},{13,9},{2,6},{6,2},{1... | collective-permute-start | bytes 786440 | tf_op jit(solution)/shard_map/ppermute | solution.py:200
  133.5 11.7 %collective-permute-start.27 = (f32[2,256,128]{2,1,0:T(8,128)S(1)}, f32[2,256,128]{2,1,0:T(8,128)S(1)}, u32[]{:S(2)}, u32[]{:S(2)}) collective-permute-start(f32[2,256,128]{2,1,0:T(8,128)S(1)} %get-tuple-element.178), channel_id=1, source_target_pairs={{4,8},{8,4},{5,9},{9,5},{6,10},{10,6},{7,11},{11,7},{20,24},{24,20... | collective-permute-start | bytes 786440 | tf_op jit(solution)/shard_map/ppermute | solution.py:199
  134.2 17.7 %collective-permute-start.37 = (f32[2,256,128]{2,1,0:T(8,128)S(1)}, f32[2,256,128]{2,1,0:T(8,128)S(1)}, u32[]{:S(2)}, u32[]{:S(2)}) collective-permute-start(f32[2,256,128]{2,1,0:T(8,128)S(1)} %get-tuple-element.169), channel_id=1, source_target_pairs={{4,8},{8,4},{5,9},{9,5},{6,10},{10,6},{7,11},{11,7},{20,24},{24,20... | collective-permute-start | bytes 786440 | tf_op jit(solution)/shard_map/ppermute | solution.py:199
  145.3 12.4 %collective-permute-start.35 = (f32[2,256,128]{2,1,0:T(8,128)S(1)}, f32[2,256,128]{2,1,0:T(8,128)S(1)}, u32[]{:S(2)}, u32[]{:S(2)}) collective-permute-start(f32[2,256,128]{2,1,0:T(8,128)S(1)} %select_select_fusion.5), channel_id=1, source_target_pairs={{0,4},{4,0},{8,12},{12,8},{1,5},{5,1},{9,13},{13,9},{2,6},{6,2},{1... | collective-permute-start | bytes 786440 | tf_op jit(solution)/shard_map/ppermute | solution.py:200
  (62 other events, 690.7 us)

commit v3 on v2

--- a/solution.py
+++ b/solution.py
@@ -12,7 +12,7 @@
 PIECES = 8
 GROUP = 2
 MINE, COLUMNS, FOLD = 1, 5, 7
-BLOCKS = {8: (0,), 9: (2, 4)}
+BLOCKS = {9: (0, 2)}
 
 
 def split(value):
@@ -272,6 +272,7 @@
             before = (result,)
         for chain in chains:
             chain.step(index, *before)
+    result = block(folded, PIECES - 2 * GROUP, chains, result)
     return block(folded, PIECES - GROUP, chains, result)
 
 

time: 166 us -> 163 us (0.982)
  other arithmetic: 16.6 us -> 22.9 us
  waiting for transfers between devices: 30 us -> 25.4 us
  starting transfers between devices: 73.1 us -> 70.9 us
  local copies, waits for them, and re-layouts: 12.9 us -> 11.2 us
    ppermute x20, waiting for transfers between devices: 28.2 us -> 24.7 us  [step(): lax.ppermute(value, 'row', [(0, 1), (1, 0), (2, 3), (3, 2)])]
    select_n x12 -> x13, other arithmetic: 5.16 us -> 8.42 us  [step(): jnp.where(self.holder, self.own[index - 1], self.outer[index - 1])]
    ppermute x20, starting transfers between devices: 58.3 us -> 55.4 us  [step(): lax.ppermute(value, 'row', [(0, 1), (1, 0), (2, 3), (3, 2)])]
    select_n x16, other arithmetic: 2.74 us -> 5.19 us  [step(): value = jnp.where(self.outside, ahead, passing)]
    unnamed x94 -> x60, local copies, waits for them, and re-layouts: 2.52 us -> 0.83 us
  transfers between devices with their start and end apart: 39 -> 39, of which waited for: 14 -> 12; matrix products, arithmetic and copies ran while one was open for 13% -> 17% of each run, Pallas kernels for 13% -> 9%
where the time goes in v3:
time: 163 us; the launch traced here: 162 us
  starting transfers between devices  70.9 us (43%)
  Pallas kernels  25.5 us (16%)
  waiting for transfers between devices  25.4 us (16%)
  other arithmetic  22.9 us (14%)
  local copies, waits for them, and re-layouts  11.2 us (7%)
  between operations  5.96 us (4%)
    ppermute x20, starting transfers between devices, step(): lax.ppermute(value, 'row', [(0, 1), (1, 0), (2, 3), (3, 2)])  55.4 us
    ppermute x20, waiting for transfers between devices, step(): lax.ppermute(value, 'row', [(0, 1), (1, 0), (2, 3), (3, 2)])  24.7 us
    pallas_call x4, Pallas kernels, block(): pl.pallas_call(block_kernel, grid=(row_count // tile,), in_specs=specs, o...  20.3 us
    ppermute x16, starting transfers between devices, step(): self.inner.append(lax.ppermute(crossing, 'row', [(1, 2), (2, 1)]))  13.5 us
    select_n x13, other arithmetic, step(): jnp.where(self.holder, self.own[index - 1], self.outer[index - 1])  8.42 us
    pallas_call x1, Pallas kernels, fold(): pl.pallas_call(fold_kernel, grid_spec=pltpu.PrefetchScalarGridSpec(num_sc...  5.24 us
    select_n x16, other arithmetic, step(): value = jnp.where(self.outside, ahead, passing)  5.19 us
    slice x1, local copies, waits for them, and re-layouts, __init__(): lax.slice_in_dim(slab, p * self.width, (p + 1) * self.width, axis=2)  3.87 us
  transfers between devices with their start and end apart: 39, of which 12 were waited for; matrix products, arithmetic and copies ran while one was open for 17% of the time, Pallas kernels for 9%

profile of v3, /device:TPU:0, one launch (start us, length us, event | category | flops | bytes accessed | tf_op | source)
XLA Modules:
  0.0 162.0 jit_solution(16358391940031162680)
XLA Ops:
  5.3 2.7 %dynamic-slice_bitcast_fusion.3 = (f32[1,2,512,256]{3,2,1,0:T(8,128)S(1)}, f32[1,2,512,256]{3,2,1,0:T(8,128)S(1)}, f32[1,2,512,256]{3,2,1,0:T(8,128)S(1)}, f32[1,2,512,256]{3,2,1,0:T(8,128)S(1)}) fusion(f32[2,1024,1024]{2,1,0:T(8,128)} %param.5, s32[]{:T(128)S(6)} %select_n.494, s32[]{:T(128)S(6)} %select_n.496, s32[]{:T(128)S(6)} %select_n.499, s32[]{:T(128)S(6)} %select_n.498), kind=kLoop, calls=%fused_computation.5 | loop fusion | bytes 8388624 | tf_op jit(solution)/shard_map/stack | solution.py:232
  10.0 3.9 %constant_dynamic-slice_fusion.14 = (f32[2,256,128]{2,1,0:T(8,128)S(1)}, f32[2,256,128]{2,1,0:T(8,128)}, f32[2,256,128]{2,1,0:T(8,128)S(1)}, f32[2,256,128]{2,1,...) fusion(f32[2,1024,1024]{2,1,0:T(8,128)} %param.5, ...), kind=kLoop, calls=%fused_computation.69 | loop fusion | bytes 8388644 | tf_op jit(solution)/shard_map/slice | solution.py:180
  13.8 2.6 %collective-permute-start.10 = (f32[2,256,128]{2,1,0:T(8,128)}, f32[2,256,128]{2,1,0:T(8,128)}, u32[]{:S(2)}, u32[]{:S(2)}) collective-permute-start(f32[2,256,128]{2,1,0:T(8,128)} %get-tuple-element.95), channel_id=1, source_target_pairs={{0,4},{4,0},{8,12},{12,8},{1,5},{5,1},{9,13},{13,9},{2,6},{6,2},{1... | collective-permute-start | bytes 786440 | tf_op jit(solution)/shard_map/ppermute | solution.py:200
  17.4 3.2 %maximum_select_fusion = f32[2,2,512,256]{3,2,1,0:T(8,128)} fusion(f32[2,2,512,256]{3,2,1,0:T(8,128)} %collective-permute-done, f32[1,2,512,256]{3,2,1,0:T(8,128)S(1)} %get-tuple-element.168, f32[1,2,512,256]{3,2,1,0:T(8,128)S(1)} %get-tuple-element.165, pred[2]{0:T(512)(128)(4,1)S(1)} %fusion), kind=kLoop, calls=%fused_computation | loop fusion | flops 1048576 | bytes 6291458 | tf_op jit(solution)/shard_map/jit(_where)/select_n | solution.py:246
  20.6 3.4 %collective-permute-done.10 = f32[2,256,128]{2,1,0:T(8,128)} collective-permute-done((f32[2,256,128]{2,1,0:T(8,128)}, f32[2,256,128]{2,1,0:T(8,128)}, u32[]{:S(2)}, u32[]{:S(2)}) %collective-permute-start.10) | collective-permute-done | bytes 262176 | tf_op jit(solution)/shard_map/ppermute | solution.py:200
  27.0 4.1 %collective-permute-start.11 = (f32[2,256,128]{2,1,0:T(8,128)}, f32[2,256,128]{2,1,0:T(8,128)}, u32[]{:S(2)}, u32[]{:S(2)}) collective-permute-start(f32[2,256,128]{2,1,0:T(8,128)} %get-tuple-element.96), channel_id=1, source_target_pairs={{0,4},{4,0},{8,12},{12,8},{1,5},{5,1},{9,13},{13,9},{2,6},{6,2},{1... | collective-permute-start | bytes 786440 | tf_op jit(solution)/shard_map/ppermute | solution.py:200
  40.4 2.8 %collective-permute-start.13 = (f32[2,256,128]{2,1,0:T(8,128)S(1)}, f32[2,256,128]{2,1,0:T(8,128)S(1)}, u32[]{:S(2)}, u32[]{:S(2)}) collective-permute-start(f32[2,256,128]{2,1,0:T(8,128)S(1)} %select_select_fusion.28), channel_id=1, source_target_pairs={{0,4},{4,0},{8,12},{12,8},{1,5},{5,1},{9,13},{13,9},{2,6},{6,2},{1... | collective-permute-start | bytes 786440 | tf_op jit(solution)/shard_map/ppermute | solution.py:200
  45.1 3.9 %collective-permute-start.5 = (f32[2,256,128]{2,1,0:T(8,128)S(1)}, f32[2,256,128]{2,1,0:T(8,128)S(1)}, u32[]{:S(2)}, u32[]{:S(2)}) collective-permute-start(f32[2,256,128]{2,1,0:T(8,128)S(1)} %select_select_fusion.31), channel_id=1, source_target_pairs={{0,4},{4,0},{8,12},{12,8},{1,5},{5,1},{9,13},{13,9},{2,6},{6,2},{1... | collective-permute-start | bytes 786440 | tf_op jit(solution)/shard_map/ppermute | solution.py:200
  53.0 3.5 %collective-permute-start.15 = (f32[2,256,128]{2,1,0:T(8,128)}, f32[2,256,128]{2,1,0:T(8,128)}, u32[]{:S(2)}, u32[]{:S(2)}) collective-permute-start(f32[2,256,128]{2,1,0:T(8,128)} %select_select_fusion.27), channel_id=1, source_target_pairs={{0,4},{4,0},{8,12},{12,8},{1,5},{5,1},{9,13},{13,9},{2,6},{6,2},{1... | collective-permute-start | bytes 786440 | tf_op jit(solution)/shard_map/ppermute | solution.py:200
  78.7 2.8 %broadcast_select_fusion.own_ref = f32[2,2,512,256]{3,2,1,0:T(8,128)S(1)} fusion(f32[2,2,512,256]{3,2,1,0:T(8,128)} %collective-permute-done.1, pred[2]{0:T(512)(128)(4,1)S(1)} %get-tuple-element.147, f32[2,2,512,256]{3,2,1,0:T(8,128)} %collective-permute-done, f32[1,2,512,256]{3,2,1,0:T(8,128)S(1)} %get-tuple-element.168, ...), kind=kLoop, calls=%fused_computation.6 | loop fusion | flops 1572864 | bytes 8388612 | tf_op jit(solution)/shard_map/jit(_where)/select_n | solution.py:264
  85.5 6.7 %collective-permute-start.20 = (f32[2,256,128]{2,1,0:T(8,128)S(1)}, f32[2,256,128]{2,1,0:T(8,128)S(1)}, u32[]{:S(2)}, u32[]{:S(2)}) collective-permute-start(f32[2,256,128]{2,1,0:T(8,128)S(1)} %select_select_fusion.25), channel_id=1, source_target_pairs={{0,4},{4,0},{8,12},{12,8},{1,5},{5,1},{9,13},{13,9},{2,6},{6,2},{1... | collective-permute-start | bytes 786440 | tf_op jit(solution)/shard_map/ppermute | solution.py:200
  92.2 3.9 %collective-permute-start.32 = (f32[2,256,128]{2,1,0:T(8,128)S(1)}, f32[2,256,128]{2,1,0:T(8,128)S(1)}, u32[]{:S(2)}, u32[]{:S(2)}) collective-permute-start(f32[2,256,128]{2,1,0:T(8,128)S(1)} %select_select_fusion.9), channel_id=1, source_target_pairs={{0,4},{4,0},{8,12},{12,8},{1,5},{5,1},{9,13},{13,9},{2,6},{6,2},{1... | collective-permute-start | bytes 786440 | tf_op jit(solution)/shard_map/ppermute | solution.py:200
  101.1 3.8 %collective-permute-start.22 = (f32[2,256,128]{2,1,0:T(8,128)S(1)}, f32[2,256,128]{2,1,0:T(8,128)S(1)}, u32[]{:S(2)}, u32[]{:S(2)}) collective-permute-start(f32[2,256,128]{2,1,0:T(8,128)S(1)} %select_select_fusion.24), channel_id=1, source_target_pairs={{0,4},{4,0},{8,12},{12,8},{1,5},{5,1},{9,13},{13,9},{2,6},{6,2},{1... | collective-permute-start | bytes 786440 | tf_op jit(solution)/shard_map/ppermute | solution.py:200
  104.9 5.2 %fold.1 = (bf16[1024,1024]{1,0:T(8,128)(2,1)S(1)}, bf16[1024,1024]{1,0:T(8,128)(2,1)S(1)}) custom-call(s32[18]{0:T(128)S(1)} %pad_add_fusion.numbers, f32[2,2,512,256]{3,2,1,0:T(8,128)S(1)} %broadcast_select_fusion.own_ref, f32[2,2,512,256]{3,2,1,0:T(8,128)S(1)} %collective-permute-done.18.other_ref, f32[2,2,64,256]{3,2,1,0:T(8,128)S(1)} %tile.10.op_ref), custom_call_target="tpu_custom_call" | custom-call | flops 6442450944 | bytes 8388608 | tf_op jit(solution)/shard_map/fold/pallas_call | solution.py:76
  110.9 2.9 %collective-permute-start.34 = (f32[2,256,128]{2,1,0:T(8,128)S(1)}, f32[2,256,128]{2,1,0:T(8,128)S(1)}, u32[]{:S(2)}, u32[]{:S(2)}) collective-permute-start(f32[2,256,128]{2,1,0:T(8,128)S(1)} %select_select_fusion.8), channel_id=1, source_target_pairs={{0,4},{4,0},{8,12},{12,8},{1,5},{5,1},{9,13},{13,9},{2,6},{6,2},{1... | collective-permute-start | bytes 786440 | tf_op jit(solution)/shard_map/ppermute | solution.py:200
  116.7 5.1 %block.4.refs_4_ = f32[2,1024,1024]{2,1,0:T(8,128)} custom-call(bf16[1024,1024]{1,0:T(8,128)(2,1)S(1)} %get-tuple-element.107.upper_ref, bf16[1024,1024]{1,0:T(8,128)(2,1)S(1)} %get-tuple-element.108.lower_ref, f32[2,256,128]{2,1,0:T(8,128)S(1)} %get-tuple-element.186.refs_0_, f32[2,256,128]{2,1,0:T(8,128)S(1)} %get-tuple-element.183.refs_1_, ...), custom_call_target="tpu_custom_call" | custom-call | flops 3221225472 | bytes 6291456 | tf_op jit(solution)/shard_map/block/pallas_call | solution.py:143
  121.7 5.1 %block.5.refs_4_ = f32[2,1024,1024]{2,1,0:T(8,128)} custom-call(bf16[1024,1024]{1,0:T(8,128)(2,1)S(1)} %get-tuple-element.107.upper_ref, bf16[1024,1024]{1,0:T(8,128)(2,1)S(1)} %get-tuple-element.108.lower_ref, f32[2,256,128]{2,1,0:T(8,128)S(1)} %get-tuple-element.187.refs_0_, ...), custom_call_target="tpu_custom_call", output_to_operand_aliasing={{}: (6, {})} | custom-call | flops 3221225472 | bytes 6291456 | tf_op jit(solution)/shard_map/block/pallas_call | solution.py:143
  127.6 2.6 %collective-permute-start.36 = (f32[2,256,128]{2,1,0:T(8,128)S(1)}, f32[2,256,128]{2,1,0:T(8,128)S(1)}, u32[]{:S(2)}, u32[]{:S(2)}) collective-permute-start(f32[2,256,128]{2,1,0:T(8,128)S(1)} %select_select_fusion.7), channel_id=1, source_target_pairs={{0,4},{4,0},{8,12},{12,8},{1,5},{5,1},{9,13},{13,9},{2,6},{6,2},{1... | collective-permute-start | bytes 786440 | tf_op jit(solution)/shard_map/ppermute | solution.py:200
  133.2 4.2 %collective-permute-done.36 = f32[2,256,128]{2,1,0:T(8,128)S(1)} collective-permute-done((f32[2,256,128]{2,1,0:T(8,128)S(1)}, f32[2,256,128]{2,1,0:T(8,128)S(1)}, u32[]{:S(2)}, u32[]{:S(2)}) %collective-permute-start.36) | collective-permute-done | bytes 262176 | tf_op jit(solution)/shard_map/ppermute | solution.py:200
  139.7 3.4 %collective-permute-done.26 = f32[2,256,128]{2,1,0:T(8,128)S(1)} collective-permute-done((f32[2,256,128]{2,1,0:T(8,128)S(1)}, f32[2,256,128]{2,1,0:T(8,128)S(1)}, u32[]{:S(2)}, u32[]{:S(2)}) %collective-permute-start.26) | collective-permute-done | bytes 262176 | tf_op jit(solution)/shard_map/ppermute | solution.py:200
  145.3 3.4 %collective-permute-done.38 = f32[2,256,128]{2,1,0:T(8,128)S(1)} collective-permute-done((f32[2,256,128]{2,1,0:T(8,128)S(1)}, f32[2,256,128]{2,1,0:T(8,128)S(1)}, u32[]{:S(2)}, u32[]{:S(2)}) %collective-permute-start.38) | collective-permute-done | bytes 262176 | tf_op jit(solution)/shard_map/ppermute | solution.py:200
  148.8 3.0 %collective-permute-done.31 = f32[2,256,128]{2,1,0:T(8,128)S(1)} collective-permute-done((f32[2,256,128]{2,1,0:T(8,128)S(1)}, f32[2,256,128]{2,1,0:T(8,128)S(1)}, u32[]{:S(2)}, u32[]{:S(2)}) %collective-permute-start.31) | collective-permute-done | bytes 262176 | tf_op jit(solution)/shard_map/ppermute | solution.py:200
  151.8 5.1 %block.6.refs_4_ = f32[2,1024,1024]{2,1,0:T(8,128)} custom-call(bf16[1024,1024]{1,0:T(8,128)(2,1)S(1)} %get-tuple-element.107.upper_ref, bf16[1024,1024]{1,0:T(8,128)(2,1)S(1)} %get-tuple-element.108.lower_ref, f32[2,256,128]{2,1,0:T(8,128)S(1)} %get-tuple-element.175.refs_0_, ...), custom_call_target="tpu_custom_call", output_to_operand_aliasing={{}: (6, {})} | custom-call | flops 3221225472 | bytes 6291456 | tf_op jit(solution)/shard_map/block/pallas_call | solution.py:143
  156.9 5.1 %block.7 = f32[2,1024,1024]{2,1,0:T(8,128)} custom-call(bf16[1024,1024]{1,0:T(8,128)(2,1)S(1)} %get-tuple-element.107.upper_ref, bf16[1024,1024]{1,0:T(8,128)(2,1)S(1)} %get-tuple-element.108.lower_ref, f32[2,256,128]{2,1,0:T(8,128)S(1)} %get-tuple-element.176.refs_0_, ...), custom_call_target="tpu_custom_call", output_to_operand_aliasing={{}: (6, {})} | custom-call | flops 3221225472 | bytes 6291456 | tf_op jit(solution)/shard_map/block/pallas_call | solution.py:143
  (168 shorter events, 63.7 us)
Async XLA Ops:
  16.5 17.0 %collective-permute-start.2 = (f32[2,256,128]{2,1,0:T(8,128)}, f32[2,256,128]{2,1,0:T(8,128)}, u32[]{:S(2)}, u32[]{:S(2)}) collective-permute-start(f32[2,256,128]{2,1,0:T(8,128)} %get-tuple-element.80), channel_id=1, source_target_pairs={{0,4},{4,0},{8,12},{12,8},{1,5},{5,1},{9,13},{13,9},{2,6},{6,2},{1... | collective-permute-start | bytes 786440 | tf_op jit(solution)/shard_map/ppermute | solution.py:200
  25.7 11.9 %collective-permute-start.12 = (f32[2,256,128]{2,1,0:T(8,128)}, f32[2,256,128]{2,1,0:T(8,128)}, u32[]{:S(2)}, u32[]{:S(2)}) collective-permute-start(f32[2,256,128]{2,1,0:T(8,128)} %broadcast_select_fusion.8), channel_id=1, source_target_pairs={{4,8},{8,4},{5,9},{9,5},{6,10},{10,6},{7,11},{11,7},{20,24},{24,20... | collective-permute-start | bytes 786440 | tf_op jit(solution)/shard_map/ppermute | solution.py:199
  27.0 10.6 %collective-permute-start.11 = (f32[2,256,128]{2,1,0:T(8,128)}, f32[2,256,128]{2,1,0:T(8,128)}, u32[]{:S(2)}, u32[]{:S(2)}) collective-permute-start(f32[2,256,128]{2,1,0:T(8,128)} %get-tuple-element.96), channel_id=1, source_target_pairs={{0,4},{4,0},{8,12},{12,8},{1,5},{5,1},{9,13},{13,9},{2,6},{6,2},{1... | collective-permute-start | bytes 786440 | tf_op jit(solution)/shard_map/ppermute | solution.py:200
  32.0 46.7 %collective-permute-start.1 = (f32[2,2,512,256]{3,2,1,0:T(8,128)}, f32[2,2,512,256]{3,2,1,0:T(8,128)}, u32[]{:S(2)}, u32[]{:S(2)}) collective-permute-start(f32[2,2,512,256]{3,2,1,0:T(8,128)} %maximum_select_fusion), channel_id=1, source_target_pairs={{0,2},{2,0},{1,3},{3,1},{4,6},{6,4},{5,7},{7,5},{8,10},{10,8},{9,1... | collective-permute-start | bytes 6291464 | tf_op jit(solution)/shard_map/ppermute | solution.py:247
  38.6 10.4 %collective-permute-start.14 = (f32[2,256,128]{2,1,0:T(8,128)S(1)}, f32[2,256,128]{2,1,0:T(8,128)S(1)}, u32[]{:S(2)}, u32[]{:S(2)}) collective-permute-start(f32[2,256,128]{2,1,0:T(8,128)S(1)} %broadcast_select_fusion.7), channel_id=1, source_target_pairs={{4,8},{8,4},{5,9},{9,5},{6,10},{10,6},{7,11},{11,7},{20,24},{24,20... | collective-permute-start | bytes 786440 | tf_op jit(solution)/shard_map/ppermute | solution.py:199
  44.3 12.2 %collective-permute-start.6 = (f32[2,256,128]{2,1,0:T(8,128)S(1)}, f32[2,256,128]{2,1,0:T(8,128)S(1)}, u32[]{:S(2)}, u32[]{:S(2)}) collective-permute-start(f32[2,256,128]{2,1,0:T(8,128)S(1)} %broadcast_select_fusion.15), channel_id=1, source_target_pairs={{4,8},{8,4},{5,9},{9,5},{6,10},{10,6},{7,11},{11,7},{20,24},{24,20... | collective-permute-start | bytes 786440 | tf_op jit(solution)/shard_map/ppermute | solution.py:199
  45.1 11.5 %collective-permute-start.5 = (f32[2,256,128]{2,1,0:T(8,128)S(1)}, f32[2,256,128]{2,1,0:T(8,128)S(1)}, u32[]{:S(2)}, u32[]{:S(2)}) collective-permute-start(f32[2,256,128]{2,1,0:T(8,128)S(1)} %select_select_fusion.31), channel_id=1, source_target_pairs={{0,4},{4,0},{8,12},{12,8},{1,5},{5,1},{9,13},{13,9},{2,6},{6,2},{1... | collective-permute-start | bytes 786440 | tf_op jit(solution)/shard_map/ppermute | solution.py:200
  50.9 12.5 %collective-permute-start.16 = (f32[2,256,128]{2,1,0:T(8,128)}, f32[2,256,128]{2,1,0:T(8,128)}, u32[]{:S(2)}, u32[]{:S(2)}) collective-permute-start(f32[2,256,128]{2,1,0:T(8,128)} %broadcast_select_fusion.6), channel_id=1, source_target_pairs={{4,8},{8,4},{5,9},{9,5},{6,10},{10,6},{7,11},{11,7},{20,24},{24,20... | collective-permute-start | bytes 786440 | tf_op jit(solution)/shard_map/ppermute | solution.py:199
  53.0 10.7 %collective-permute-start.15 = (f32[2,256,128]{2,1,0:T(8,128)}, f32[2,256,128]{2,1,0:T(8,128)}, u32[]{:S(2)}, u32[]{:S(2)}) collective-permute-start(f32[2,256,128]{2,1,0:T(8,128)} %select_select_fusion.27), channel_id=1, source_target_pairs={{0,4},{4,0},{8,12},{12,8},{1,5},{5,1},{9,13},{13,9},{2,6},{6,2},{1... | collective-permute-start | bytes 786440 | tf_op jit(solution)/shard_map/ppermute | solution.py:200
  64.7 11.2 %collective-permute-start.17 = (f32[2,256,128]{2,1,0:T(8,128)S(1)}, f32[2,256,128]{2,1,0:T(8,128)S(1)}, u32[]{:S(2)}, u32[]{:S(2)}) collective-permute-start(f32[2,256,128]{2,1,0:T(8,128)S(1)} %select_select_fusion.26), channel_id=1, source_target_pairs={{0,4},{4,0},{8,12},{12,8},{1,5},{5,1},{9,13},{13,9},{2,6},{6,2},{1... | collective-permute-start | bytes 786440 | tf_op jit(solution)/shard_map/ppermute | solution.py:200
  81.5 23.4 %collective-permute-start.18 = (f32[2,2,512,256]{3,2,1,0:T(8,128)S(1)}, f32[2,2,512,256]{3,2,1,0:T(8,128)S(1)}, u32[]{:S(2)}, u32[]{:S(2)}) collective-permute-start(f32[2,2,512,256]{3,2,1,0:T(8,128)S(1)} %broadcast_select_fusion.own_ref), channel_id=1, source_target_pairs={{0,1},{1,0},{2,3},{3,2},{4,5},{5,4},{6,7},{7,6},{8,9},{9,8},{10,11... | collective-permute-start | bytes 6291464 | tf_op jit(solution)/shard_map/ppermute | solution.py:267
  81.6 10.5 %collective-permute-start.29 = (f32[2,256,128]{2,1,0:T(8,128)S(1)}, f32[2,256,128]{2,1,0:T(8,128)S(1)}, u32[]{:S(2)}, u32[]{:S(2)}) collective-permute-start(f32[2,256,128]{2,1,0:T(8,128)S(1)} %select_select_fusion.18), channel_id=1, source_target_pairs={{0,4},{4,0},{8,12},{12,8},{1,5},{5,1},{9,13},{13,9},{2,6},{6,2},{1... | collective-permute-start | bytes 786440 | tf_op jit(solution)/shard_map/ppermute | solution.py:200
  84.7 13.3 %collective-permute-start.21 = (f32[2,256,128]{2,1,0:T(8,128)S(1)}, f32[2,256,128]{2,1,0:T(8,128)S(1)}, u32[]{:S(2)}, u32[]{:S(2)}) collective-permute-start(f32[2,256,128]{2,1,0:T(8,128)S(1)} %get-tuple-element.188), channel_id=1, source_target_pairs={{4,8},{8,4},{5,9},{9,5},{6,10},{10,6},{7,11},{11,7},{20,24},{24,20... | collective-permute-start | bytes 786440 | tf_op jit(solution)/shard_map/ppermute | solution.py:199
  85.5 13.8 %collective-permute-start.20 = (f32[2,256,128]{2,1,0:T(8,128)S(1)}, f32[2,256,128]{2,1,0:T(8,128)S(1)}, u32[]{:S(2)}, u32[]{:S(2)}) collective-permute-start(f32[2,256,128]{2,1,0:T(8,128)S(1)} %select_select_fusion.25), channel_id=1, source_target_pairs={{0,4},{4,0},{8,12},{12,8},{1,5},{5,1},{9,13},{13,9},{2,6},{6,2},{1... | collective-permute-start | bytes 786440 | tf_op jit(solution)/shard_map/ppermute | solution.py:200
  92.2 17.9 %collective-permute-start.32 = (f32[2,256,128]{2,1,0:T(8,128)S(1)}, f32[2,256,128]{2,1,0:T(8,128)S(1)}, u32[]{:S(2)}, u32[]{:S(2)}) collective-permute-start(f32[2,256,128]{2,1,0:T(8,128)S(1)} %select_select_fusion.9), channel_id=1, source_target_pairs={{0,4},{4,0},{8,12},{12,8},{1,5},{5,1},{9,13},{13,9},{2,6},{6,2},{1... | collective-permute-start | bytes 786440 | tf_op jit(solution)/shard_map/ppermute | solution.py:200
  97.2 12.9 %collective-permute-start.33 = (f32[2,256,128]{2,1,0:T(8,128)S(1)}, f32[2,256,128]{2,1,0:T(8,128)S(1)}, u32[]{:S(2)}, u32[]{:S(2)}) collective-permute-start(f32[2,256,128]{2,1,0:T(8,128)S(1)} %get-tuple-element.177), channel_id=1, source_target_pairs={{4,8},{8,4},{5,9},{9,5},{6,10},{10,6},{7,11},{11,7},{20,24},{24,20... | collective-permute-start | bytes 786440 | tf_op jit(solution)/shard_map/ppermute | solution.py:199
  100.4 13.5 %collective-permute-start.23 = (f32[2,256,128]{2,1,0:T(8,128)S(1)}, f32[2,256,128]{2,1,0:T(8,128)S(1)}, u32[]{:S(2)}, u32[]{:S(2)}) collective-permute-start(f32[2,256,128]{2,1,0:T(8,128)S(1)} %get-tuple-element.185), channel_id=1, source_target_pairs={{4,8},{8,4},{5,9},{9,5},{6,10},{10,6},{7,11},{11,7},{20,24},{24,20... | collective-permute-start | bytes 786440 | tf_op jit(solution)/shard_map/ppermute | solution.py:199
  101.1 12.8 %collective-permute-start.22 = (f32[2,256,128]{2,1,0:T(8,128)S(1)}, f32[2,256,128]{2,1,0:T(8,128)S(1)}, u32[]{:S(2)}, u32[]{:S(2)}) collective-permute-start(f32[2,256,128]{2,1,0:T(8,128)S(1)} %select_select_fusion.24), channel_id=1, source_target_pairs={{0,4},{4,0},{8,12},{12,8},{1,5},{5,1},{9,13},{13,9},{2,6},{6,2},{1... | collective-permute-start | bytes 786440 | tf_op jit(solution)/shard_map/ppermute | solution.py:200
  110.2 16.6 %collective-permute-start.35 = (f32[2,256,128]{2,1,0:T(8,128)S(1)}, f32[2,256,128]{2,1,0:T(8,128)S(1)}, u32[]{:S(2)}, u32[]{:S(2)}) collective-permute-start(f32[2,256,128]{2,1,0:T(8,128)S(1)} %broadcast_select_fusion.2), channel_id=1, source_target_pairs={{4,8},{8,4},{5,9},{9,5},{6,10},{10,6},{7,11},{11,7},{20,24},{24,20... | collective-permute-start | bytes 786440 | tf_op jit(solution)/shard_map/ppermute | solution.py:199
  110.9 15.9 %collective-permute-start.34 = (f32[2,256,128]{2,1,0:T(8,128)S(1)}, f32[2,256,128]{2,1,0:T(8,128)S(1)}, u32[]{:S(2)}, u32[]{:S(2)}) collective-permute-start(f32[2,256,128]{2,1,0:T(8,128)S(1)} %select_select_fusion.8), channel_id=1, source_target_pairs={{0,4},{4,0},{8,12},{12,8},{1,5},{5,1},{9,13},{13,9},{2,6},{6,2},{1... | collective-permute-start | bytes 786440 | tf_op jit(solution)/shard_map/ppermute | solution.py:200
  113.9 16.3 %collective-permute-start.25 = (f32[2,256,128]{2,1,0:T(8,128)S(1)}, f32[2,256,128]{2,1,0:T(8,128)S(1)}, u32[]{:S(2)}, u32[]{:S(2)}) collective-permute-start(f32[2,256,128]{2,1,0:T(8,128)S(1)} %broadcast_select_fusion.10), channel_id=1, source_target_pairs={{4,8},{8,4},{5,9},{9,5},{6,10},{10,6},{7,11},{11,7},{20,24},{24,20... | collective-permute-start | bytes 786440 | tf_op jit(solution)/shard_map/ppermute | solution.py:199
  114.6 15.6 %collective-permute-start.24 = (f32[2,256,128]{2,1,0:T(8,128)S(1)}, f32[2,256,128]{2,1,0:T(8,128)S(1)}, u32[]{:S(2)}, u32[]{:S(2)}) collective-permute-start(f32[2,256,128]{2,1,0:T(8,128)S(1)} %select_select_fusion.23), channel_id=1, source_target_pairs={{0,4},{4,0},{8,12},{12,8},{1,5},{5,1},{9,13},{13,9},{2,6},{6,2},{1... | collective-permute-start | bytes 786440 | tf_op jit(solution)/shard_map/ppermute | solution.py:200
  131.2 11.9 %collective-permute-start.26 = (f32[2,256,128]{2,1,0:T(8,128)S(1)}, f32[2,256,128]{2,1,0:T(8,128)S(1)}, u32[]{:S(2)}, u32[]{:S(2)}) collective-permute-start(f32[2,256,128]{2,1,0:T(8,128)S(1)} %select_select_fusion.22), channel_id=1, source_target_pairs={{0,4},{4,0},{8,12},{12,8},{1,5},{5,1},{9,13},{13,9},{2,6},{6,2},{1... | collective-permute-start | bytes 786440 | tf_op jit(solution)/shard_map/ppermute | solution.py:200
  137.5 11.2 %collective-permute-start.38 = (f32[2,256,128]{2,1,0:T(8,128)S(1)}, f32[2,256,128]{2,1,0:T(8,128)S(1)}, u32[]{:S(2)}, u32[]{:S(2)}) collective-permute-start(f32[2,256,128]{2,1,0:T(8,128)S(1)} %select_select_fusion.5), channel_id=1, source_target_pairs={{0,4},{4,0},{8,12},{12,8},{1,5},{5,1},{9,13},{13,9},{2,6},{6,2},{1... | collective-permute-start | bytes 786440 | tf_op jit(solution)/shard_map/ppermute | solution.py:200
  (45 other events, 449.8 us)

commit v4 on v3

--- a/solution.py
+++ b/solution.py
@@ -262,7 +262,6 @@
         elif index == COLUMNS:
             came = tie(across, *[chain.outer[-1] for chain in chains])
             chosen = jnp.where((owner // spin_size == side)[:, None, None, None], mine, came)
-            before = (chosen,)
         elif index == FOLD:
             other = lax.ppermute(chosen, "spin", exchange)
             before = folded = fold(settings, chosen, other, ops)

time: 163 us -> 162 us (level)
  waiting for transfers between devices: 25.4 us -> 23.7 us
    ppermute x20, waiting for transfers between devices: 24.7 us -> 22.2 us  [step(): lax.ppermute(value, 'row', [(0, 1), (1, 0), (2, 3), (3, 2)])]
    select_n x13, other arithmetic: 8.42 us -> 6.68 us  [step(): jnp.where(self.holder, self.own[index - 1], self.outer[index - 1])]
  transfers between devices with their start and end apart: 39 -> 39, of which waited for: 12 -> 11; matrix products, arithmetic and copies ran while one was open for 17% -> 17% of each run, Pallas kernels for 9% -> 10%
where the time goes in v4:
time: 162 us; the launch traced here: 161 us
  starting transfers between devices  70.9 us (44%)
  Pallas kernels  25.5 us (16%)
  waiting for transfers between devices  23.7 us (15%)
  other arithmetic  22.3 us (14%)
  local copies, waits for them, and re-layouts  12.6 us (8%)
  between operations  5.92 us (4%)
    ppermute x20, starting transfers between devices, step(): lax.ppermute(value, 'row', [(0, 1), (1, 0), (2, 3), (3, 2)])  56 us
    ppermute x20, waiting for transfers between devices, step(): lax.ppermute(value, 'row', [(0, 1), (1, 0), (2, 3), (3, 2)])  22.2 us
    pallas_call x4, Pallas kernels, block(): pl.pallas_call(block_kernel, grid=(row_count // tile,), in_specs=specs, o...  20.3 us
    ppermute x16, starting transfers between devices, step(): self.inner.append(lax.ppermute(crossing, 'row', [(1, 2), (2, 1)]))  12.9 us
    select_n x13, other arithmetic, step(): jnp.where(self.holder, self.own[index - 1], self.outer[index - 1])  6.68 us
    pallas_call x1, Pallas kernels, fold(): pl.pallas_call(fold_kernel, grid_spec=pltpu.PrefetchScalarGridSpec(num_sc...  5.24 us
    select_n x16, other arithmetic, step(): value = jnp.where(self.outside, ahead, passing)  5.15 us
    slice x1, local copies, waits for them, and re-layouts, __init__(): lax.slice_in_dim(slab, p * self.width, (p + 1) * self.width, axis=2)  3.82 us
  transfers between devices with their start and end apart: 39, of which 11 were waited for; matrix products, arithmetic and copies ran while one was open for 17% of the time, Pallas kernels for 10%

profile of v4, /device:TPU:0, one launch (start us, length us, event | category | flops | bytes accessed | tf_op | source)
XLA Modules:
  0.0 161.0 jit_solution(10942089871684643782)
XLA Ops:
  5.2 2.7 %dynamic-slice_bitcast_fusion.3 = (f32[1,2,512,256]{3,2,1,0:T(8,128)S(1)}, f32[1,2,512,256]{3,2,1,0:T(8,128)S(1)}, f32[1,2,512,256]{3,2,1,0:T(8,128)S(1)}, f32[1,2,512,256]{3,2,1,0:T(8,128)S(1)}) fusion(f32[2,1024,1024]{2,1,0:T(8,128)} %param.5, s32[]{:T(128)S(6)} %select_n.494, s32[]{:T(128)S(6)} %select_n.496, s32[]{:T(128)S(6)} %select_n.499, s32[]{:T(128)S(6)} %select_n.498), kind=kLoop, calls=%fused_computation.5 | loop fusion | bytes 8388624 | tf_op jit(solution)/shard_map/stack | solution.py:232
  9.9 3.8 %constant_dynamic-slice_fusion.14 = (f32[2,256,128]{2,1,0:T(8,128)S(1)}, f32[2,256,128]{2,1,0:T(8,128)}, f32[2,256,128]{2,1,0:T(8,128)S(1)}, f32[2,256,128]{2,1,...) fusion(f32[2,1024,1024]{2,1,0:T(8,128)} %param.5, ...), kind=kLoop, calls=%fused_computation.69 | loop fusion | bytes 8388644 | tf_op jit(solution)/shard_map/slice | solution.py:180
  17.2 3.2 %maximum_select_fusion = f32[2,2,512,256]{3,2,1,0:T(8,128)} fusion(f32[2,2,512,256]{3,2,1,0:T(8,128)} %collective-permute-done, f32[1,2,512,256]{3,2,1,0:T(8,128)S(1)} %get-tuple-element.168, f32[1,2,512,256]{3,2,1,0:T(8,128)S(1)} %get-tuple-element.165, pred[2]{0:T(512)(128)(4,1)S(1)} %fusion), kind=kLoop, calls=%fused_computation | loop fusion | flops 1048576 | bytes 6291458 | tf_op jit(solution)/shard_map/jit(_where)/select_n | solution.py:246
  20.5 3.3 %collective-permute-done.10 = f32[2,256,128]{2,1,0:T(8,128)} collective-permute-done((f32[2,256,128]{2,1,0:T(8,128)}, f32[2,256,128]{2,1,0:T(8,128)}, u32[]{:S(2)}, u32[]{:S(2)}) %collective-permute-start.10) | collective-permute-done | bytes 262176 | tf_op jit(solution)/shard_map/ppermute | solution.py:200
  26.9 4.1 %collective-permute-start.11 = (f32[2,256,128]{2,1,0:T(8,128)}, f32[2,256,128]{2,1,0:T(8,128)}, u32[]{:S(2)}, u32[]{:S(2)}) collective-permute-start(f32[2,256,128]{2,1,0:T(8,128)} %get-tuple-element.96), channel_id=1, source_target_pairs={{0,4},{4,0},{8,12},{12,8},{1,5},{5,1},{9,13},{13,9},{2,6},{6,2},{1... | collective-permute-start | bytes 786440 | tf_op jit(solution)/shard_map/ppermute | solution.py:200
  40.2 2.9 %collective-permute-start.13 = (f32[2,256,128]{2,1,0:T(8,128)S(1)}, f32[2,256,128]{2,1,0:T(8,128)S(1)}, u32[]{:S(2)}, u32[]{:S(2)}) collective-permute-start(f32[2,256,128]{2,1,0:T(8,128)S(1)} %select_select_fusion.28), channel_id=1, source_target_pairs={{0,4},{4,0},{8,12},{12,8},{1,5},{5,1},{9,13},{13,9},{2,6},{6,2},{1... | collective-permute-start | bytes 786440 | tf_op jit(solution)/shard_map/ppermute | solution.py:200
  45.8 2.9 %collective-permute-start.5 = (f32[2,256,128]{2,1,0:T(8,128)S(1)}, f32[2,256,128]{2,1,0:T(8,128)S(1)}, u32[]{:S(2)}, u32[]{:S(2)}) collective-permute-start(f32[2,256,128]{2,1,0:T(8,128)S(1)} %select_select_fusion.31), channel_id=1, source_target_pairs={{0,4},{4,0},{8,12},{12,8},{1,5},{5,1},{9,13},{13,9},{2,6},{6,2},{1... | collective-permute-start | bytes 786440 | tf_op jit(solution)/shard_map/ppermute | solution.py:200
  52.3 3.4 %collective-permute-start.15 = (f32[2,256,128]{2,1,0:T(8,128)S(1)}, f32[2,256,128]{2,1,0:T(8,128)S(1)}, u32[]{:S(2)}, u32[]{:S(2)}) collective-permute-start(f32[2,256,128]{2,1,0:T(8,128)S(1)} %select_select_fusion.27), channel_id=1, source_target_pairs={{0,4},{4,0},{8,12},{12,8},{1,5},{5,1},{9,13},{13,9},{2,6},{6,2},{1... | collective-permute-start | bytes 786440 | tf_op jit(solution)/shard_map/ppermute | solution.py:200
  57.3 3.9 %collective-permute-start.7 = (f32[2,256,128]{2,1,0:T(8,128)S(1)}, f32[2,256,128]{2,1,0:T(8,128)S(1)}, u32[]{:S(2)}, u32[]{:S(2)}) collective-permute-start(f32[2,256,128]{2,1,0:T(8,128)S(1)} %select_select_fusion.30), channel_id=1, source_target_pairs={{0,4},{4,0},{8,12},{12,8},{1,5},{5,1},{9,13},{13,9},{2,6},{6,2},{1... | collective-permute-start | bytes 786440 | tf_op jit(solution)/shard_map/ppermute | solution.py:200
  65.1 3.3 %collective-permute-start.17 = (f32[2,256,128]{2,1,0:T(8,128)}, f32[2,256,128]{2,1,0:T(8,128)}, u32[]{:S(2)}, u32[]{:S(2)}) collective-permute-start(f32[2,256,128]{2,1,0:T(8,128)} %select_select_fusion.26), channel_id=1, source_target_pairs={{0,4},{4,0},{8,12},{12,8},{1,5},{5,1},{9,13},{13,9},{2,6},{6,2},{1... | collective-permute-start | bytes 786440 | tf_op jit(solution)/shard_map/ppermute | solution.py:200
  78.5 2.8 %broadcast_select_fusion.own_ref = f32[2,2,512,256]{3,2,1,0:T(8,128)S(1)} fusion(f32[2,2,512,256]{3,2,1,0:T(8,128)} %collective-permute-done.1, pred[2]{0:T(512)(128)(4,1)S(1)} %get-tuple-element.147, f32[2,2,512,256]{3,2,1,0:T(8,128)} %collective-permute-done, f32[1,2,512,256]{3,2,1,0:T(8,128)S(1)} %get-tuple-element.168, ...), kind=kLoop, calls=%fused_computation.6 | loop fusion | flops 1572864 | bytes 8388612 | tf_op jit(solution)/shard_map/jit(_where)/select_n | solution.py:264
  87.1 5.0 %collective-permute-start.20 = (f32[2,256,128]{2,1,0:T(8,128)S(1)}, f32[2,256,128]{2,1,0:T(8,128)S(1)}, u32[]{:S(2)}, u32[]{:S(2)}) collective-permute-start(f32[2,256,128]{2,1,0:T(8,128)S(1)} %select_select_fusion.25), channel_id=1, source_target_pairs={{0,4},{4,0},{8,12},{12,8},{1,5},{5,1},{9,13},{13,9},{2,6},{6,2},{1... | collective-permute-start | bytes 786440 | tf_op jit(solution)/shard_map/ppermute | solution.py:200
  92.1 3.9 %collective-permute-start.32 = (f32[2,256,128]{2,1,0:T(8,128)S(1)}, f32[2,256,128]{2,1,0:T(8,128)S(1)}, u32[]{:S(2)}, u32[]{:S(2)}) collective-permute-start(f32[2,256,128]{2,1,0:T(8,128)S(1)} %select_select_fusion.9), channel_id=1, source_target_pairs={{0,4},{4,0},{8,12},{12,8},{1,5},{5,1},{9,13},{13,9},{2,6},{6,2},{1... | collective-permute-start | bytes 786440 | tf_op jit(solution)/shard_map/ppermute | solution.py:200
  100.1 4.9 %collective-permute-start.22 = (f32[2,256,128]{2,1,0:T(8,128)S(1)}, f32[2,256,128]{2,1,0:T(8,128)S(1)}, u32[]{:S(2)}, u32[]{:S(2)}) collective-permute-start(f32[2,256,128]{2,1,0:T(8,128)S(1)} %select_select_fusion.24), channel_id=1, source_target_pairs={{0,4},{4,0},{8,12},{12,8},{1,5},{5,1},{9,13},{13,9},{2,6},{6,2},{1... | collective-permute-start | bytes 786440 | tf_op jit(solution)/shard_map/ppermute | solution.py:200
  105.1 5.2 %fold.1 = (bf16[1024,1024]{1,0:T(8,128)(2,1)S(1)}, bf16[1024,1024]{1,0:T(8,128)(2,1)S(1)}) custom-call(s32[18]{0:T(128)S(1)} %pad_add_fusion.numbers, f32[2,2,512,256]{3,2,1,0:T(8,128)S(1)} %broadcast_select_fusion.own_ref, f32[2,2,512,256]{3,2,1,0:T(8,128)S(1)} %collective-permute-done.18.other_ref, f32[2,2,64,256]{3,2,1,0:T(8,128)S(1)} %tile.10.op_ref), custom_call_target="tpu_custom_call" | custom-call | flops 6442450944 | bytes 8388608 | tf_op jit(solution)/shard_map/fold/pallas_call | solution.py:76
  113.6 2.9 %collective-permute-start.24 = (f32[2,256,128]{2,1,0:T(8,128)S(1)}, f32[2,256,128]{2,1,0:T(8,128)S(1)}, u32[]{:S(2)}, u32[]{:S(2)}) collective-permute-start(f32[2,256,128]{2,1,0:T(8,128)S(1)} %select_select_fusion.23), channel_id=1, source_target_pairs={{0,4},{4,0},{8,12},{12,8},{1,5},{5,1},{9,13},{13,9},{2,6},{6,2},{1... | collective-permute-start | bytes 786440 | tf_op jit(solution)/shard_map/ppermute | solution.py:200
  116.5 5.1 %block.4.refs_4_ = f32[2,1024,1024]{2,1,0:T(8,128)} custom-call(bf16[1024,1024]{1,0:T(8,128)(2,1)S(1)} %get-tuple-element.107.upper_ref, bf16[1024,1024]{1,0:T(8,128)(2,1)S(1)} %get-tuple-element.108.lower_ref, f32[2,256,128]{2,1,0:T(8,128)S(1)} %get-tuple-element.186.refs_0_, f32[2,256,128]{2,1,0:T(8,128)S(1)} %get-tuple-element.183.refs_1_, ...), custom_call_target="tpu_custom_call" | custom-call | flops 3221225472 | bytes 6291456 | tf_op jit(solution)/shard_map/block/pallas_call | solution.py:143
  121.6 5.1 %block.5.refs_4_ = f32[2,1024,1024]{2,1,0:T(8,128)} custom-call(bf16[1024,1024]{1,0:T(8,128)(2,1)S(1)} %get-tuple-element.107.upper_ref, bf16[1024,1024]{1,0:T(8,128)(2,1)S(1)} %get-tuple-element.108.lower_ref, f32[2,256,128]{2,1,0:T(8,128)S(1)} %get-tuple-element.187.refs_0_, ...), custom_call_target="tpu_custom_call", output_to_operand_aliasing={{}: (6, {})} | custom-call | flops 3221225472 | bytes 6291456 | tf_op jit(solution)/shard_map/block/pallas_call | solution.py:143
  133.1 3.4 %collective-permute-done.36 = f32[2,256,128]{2,1,0:T(8,128)S(1)} collective-permute-done((f32[2,256,128]{2,1,0:T(8,128)S(1)}, f32[2,256,128]{2,1,0:T(8,128)S(1)}, u32[]{:S(2)}, u32[]{:S(2)}) %collective-permute-start.36) | collective-permute-done | bytes 262176 | tf_op jit(solution)/shard_map/ppermute | solution.py:200
  138.9 3.2 %collective-permute-done.26 = f32[2,256,128]{2,1,0:T(8,128)S(1)} collective-permute-done((f32[2,256,128]{2,1,0:T(8,128)S(1)}, f32[2,256,128]{2,1,0:T(8,128)S(1)}, u32[]{:S(2)}, u32[]{:S(2)}) %collective-permute-start.26) | collective-permute-done | bytes 262176 | tf_op jit(solution)/shard_map/ppermute | solution.py:200
  144.5 3.2 %collective-permute-done.38 = f32[2,256,128]{2,1,0:T(8,128)S(1)} collective-permute-done((f32[2,256,128]{2,1,0:T(8,128)S(1)}, f32[2,256,128]{2,1,0:T(8,128)S(1)}, u32[]{:S(2)}, u32[]{:S(2)}) %collective-permute-start.38) | collective-permute-done | bytes 262176 | tf_op jit(solution)/shard_map/ppermute | solution.py:200
  147.8 2.9 %collective-permute-done.31 = f32[2,256,128]{2,1,0:T(8,128)S(1)} collective-permute-done((f32[2,256,128]{2,1,0:T(8,128)S(1)}, f32[2,256,128]{2,1,0:T(8,128)S(1)}, u32[]{:S(2)}, u32[]{:S(2)}) %collective-permute-start.31) | collective-permute-done | bytes 262176 | tf_op jit(solution)/shard_map/ppermute | solution.py:200
  150.8 5.1 %block.6.refs_4_ = f32[2,1024,1024]{2,1,0:T(8,128)} custom-call(bf16[1024,1024]{1,0:T(8,128)(2,1)S(1)} %get-tuple-element.107.upper_ref, bf16[1024,1024]{1,0:T(8,128)(2,1)S(1)} %get-tuple-element.108.lower_ref, f32[2,256,128]{2,1,0:T(8,128)S(1)} %get-tuple-element.175.refs_0_, ...), custom_call_target="tpu_custom_call", output_to_operand_aliasing={{}: (6, {})} | custom-call | flops 3221225472 | bytes 6291456 | tf_op jit(solution)/shard_map/block/pallas_call | solution.py:143
  155.9 5.1 %block.7 = f32[2,1024,1024]{2,1,0:T(8,128)} custom-call(bf16[1024,1024]{1,0:T(8,128)(2,1)S(1)} %get-tuple-element.107.upper_ref, bf16[1024,1024]{1,0:T(8,128)(2,1)S(1)} %get-tuple-element.108.lower_ref, f32[2,256,128]{2,1,0:T(8,128)S(1)} %get-tuple-element.176.refs_0_, ...), custom_call_target="tpu_custom_call", output_to_operand_aliasing={{}: (6, {})} | custom-call | flops 3221225472 | bytes 6291456 | tf_op jit(solution)/shard_map/block/pallas_call | solution.py:143
  (188 shorter events, 63.7 us)
Async XLA Ops:
  16.3 17.0 %collective-permute-start.2 = (f32[2,256,128]{2,1,0:T(8,128)}, f32[2,256,128]{2,1,0:T(8,128)}, u32[]{:S(2)}, u32[]{:S(2)}) collective-permute-start(f32[2,256,128]{2,1,0:T(8,128)} %get-tuple-element.80), channel_id=1, source_target_pairs={{0,4},{4,0},{8,12},{12,8},{1,5},{5,1},{9,13},{13,9},{2,6},{6,2},{1... | collective-permute-start | bytes 786440 | tf_op jit(solution)/shard_map/ppermute | solution.py:200
  25.5 11.9 %collective-permute-start.12 = (f32[2,256,128]{2,1,0:T(8,128)}, f32[2,256,128]{2,1,0:T(8,128)}, u32[]{:S(2)}, u32[]{:S(2)}) collective-permute-start(f32[2,256,128]{2,1,0:T(8,128)} %broadcast_select_fusion.8), channel_id=1, source_target_pairs={{4,8},{8,4},{5,9},{9,5},{6,10},{10,6},{7,11},{11,7},{20,24},{24,20... | collective-permute-start | bytes 786440 | tf_op jit(solution)/shard_map/ppermute | solution.py:199
  26.9 10.5 %collective-permute-start.11 = (f32[2,256,128]{2,1,0:T(8,128)}, f32[2,256,128]{2,1,0:T(8,128)}, u32[]{:S(2)}, u32[]{:S(2)}) collective-permute-start(f32[2,256,128]{2,1,0:T(8,128)} %get-tuple-element.96), channel_id=1, source_target_pairs={{0,4},{4,0},{8,12},{12,8},{1,5},{5,1},{9,13},{13,9},{2,6},{6,2},{1... | collective-permute-start | bytes 786440 | tf_op jit(solution)/shard_map/ppermute | solution.py:200
  31.8 46.7 %collective-permute-start.1 = (f32[2,2,512,256]{3,2,1,0:T(8,128)}, f32[2,2,512,256]{3,2,1,0:T(8,128)}, u32[]{:S(2)}, u32[]{:S(2)}) collective-permute-start(f32[2,2,512,256]{3,2,1,0:T(8,128)} %maximum_select_fusion), channel_id=1, source_target_pairs={{0,2},{2,0},{1,3},{3,1},{4,6},{6,4},{5,7},{7,5},{8,10},{10,8},{9,1... | collective-permute-start | bytes 6291464 | tf_op jit(solution)/shard_map/ppermute | solution.py:247
  44.0 11.6 %collective-permute-start.6 = (f32[2,256,128]{2,1,0:T(8,128)S(1)}, f32[2,256,128]{2,1,0:T(8,128)S(1)}, u32[]{:S(2)}, u32[]{:S(2)}) collective-permute-start(f32[2,256,128]{2,1,0:T(8,128)S(1)} %broadcast_select_fusion.15), channel_id=1, source_target_pairs={{4,8},{8,4},{5,9},{9,5},{6,10},{10,6},{7,11},{11,7},{20,24},{24,20... | collective-permute-start | bytes 786440 | tf_op jit(solution)/shard_map/ppermute | solution.py:199
  50.6 10.6 %collective-permute-start.16 = (f32[2,256,128]{2,1,0:T(8,128)S(1)}, f32[2,256,128]{2,1,0:T(8,128)S(1)}, u32[]{:S(2)}, u32[]{:S(2)}) collective-permute-start(f32[2,256,128]{2,1,0:T(8,128)S(1)} %broadcast_select_fusion.6), channel_id=1, source_target_pairs={{4,8},{8,4},{5,9},{9,5},{6,10},{10,6},{7,11},{11,7},{20,24},{24,20... | collective-permute-start | bytes 786440 | tf_op jit(solution)/shard_map/ppermute | solution.py:199
  56.4 12.0 %collective-permute-start.8 = (f32[2,256,128]{2,1,0:T(8,128)S(1)}, f32[2,256,128]{2,1,0:T(8,128)S(1)}, u32[]{:S(2)}, u32[]{:S(2)}) collective-permute-start(f32[2,256,128]{2,1,0:T(8,128)S(1)} %broadcast_select_fusion.14), channel_id=1, source_target_pairs={{4,8},{8,4},{5,9},{9,5},{6,10},{10,6},{7,11},{11,7},{20,24},{24,20... | collective-permute-start | bytes 786440 | tf_op jit(solution)/shard_map/ppermute | solution.py:199
  57.3 11.1 %collective-permute-start.7 = (f32[2,256,128]{2,1,0:T(8,128)S(1)}, f32[2,256,128]{2,1,0:T(8,128)S(1)}, u32[]{:S(2)}, u32[]{:S(2)}) collective-permute-start(f32[2,256,128]{2,1,0:T(8,128)S(1)} %select_select_fusion.30), channel_id=1, source_target_pairs={{0,4},{4,0},{8,12},{12,8},{1,5},{5,1},{9,13},{13,9},{2,6},{6,2},{1... | collective-permute-start | bytes 786440 | tf_op jit(solution)/shard_map/ppermute | solution.py:200
  63.0 11.5 %collective-permute-start.28 = (f32[2,256,128]{2,1,0:T(8,128)}, f32[2,256,128]{2,1,0:T(8,128)}, u32[]{:S(2)}, u32[]{:S(2)}) collective-permute-start(f32[2,256,128]{2,1,0:T(8,128)} %broadcast_select_fusion.5), channel_id=1, source_target_pairs={{4,8},{8,4},{5,9},{9,5},{6,10},{10,6},{7,11},{11,7},{20,24},{24,20... | collective-permute-start | bytes 786440 | tf_op jit(solution)/shard_map/ppermute | solution.py:199
  73.8 11.3 %collective-permute-start.19 = (f32[2,256,128]{2,1,0:T(8,128)S(1)}, f32[2,256,128]{2,1,0:T(8,128)S(1)}, u32[]{:S(2)}, u32[]{:S(2)}) collective-permute-start(f32[2,256,128]{2,1,0:T(8,128)S(1)} %broadcast_select_fusion.13), channel_id=1, source_target_pairs={{4,8},{8,4},{5,9},{9,5},{6,10},{10,6},{7,11},{11,7},{20,24},{24,20... | collective-permute-start | bytes 786440 | tf_op jit(solution)/shard_map/ppermute | solution.py:199
  81.3 23.7 %collective-permute-start.18 = (f32[2,2,512,256]{3,2,1,0:T(8,128)S(1)}, f32[2,2,512,256]{3,2,1,0:T(8,128)S(1)}, u32[]{:S(2)}, u32[]{:S(2)}) collective-permute-start(f32[2,2,512,256]{3,2,1,0:T(8,128)S(1)} %broadcast_select_fusion.own_ref), channel_id=1, source_target_pairs={{0,1},{1,0},{2,3},{3,2},{4,5},{5,4},{6,7},{7,6},{8,9},{9,8},{10,11... | collective-permute-start | bytes 6291464 | tf_op jit(solution)/shard_map/ppermute | solution.py:266
  81.5 10.6 %collective-permute-start.29 = (f32[2,256,128]{2,1,0:T(8,128)S(1)}, f32[2,256,128]{2,1,0:T(8,128)S(1)}, u32[]{:S(2)}, u32[]{:S(2)}) collective-permute-start(f32[2,256,128]{2,1,0:T(8,128)S(1)} %select_select_fusion.18), channel_id=1, source_target_pairs={{0,4},{4,0},{8,12},{12,8},{1,5},{5,1},{9,13},{13,9},{2,6},{6,2},{1... | collective-permute-start | bytes 786440 | tf_op jit(solution)/shard_map/ppermute | solution.py:200
  86.3 11.6 %collective-permute-start.21 = (f32[2,256,128]{2,1,0:T(8,128)S(1)}, f32[2,256,128]{2,1,0:T(8,128)S(1)}, u32[]{:S(2)}, u32[]{:S(2)}) collective-permute-start(f32[2,256,128]{2,1,0:T(8,128)S(1)} %get-tuple-element.188), channel_id=1, source_target_pairs={{4,8},{8,4},{5,9},{9,5},{6,10},{10,6},{7,11},{11,7},{20,24},{24,20... | collective-permute-start | bytes 786440 | tf_op jit(solution)/shard_map/ppermute | solution.py:199
  87.1 12.1 %collective-permute-start.20 = (f32[2,256,128]{2,1,0:T(8,128)S(1)}, f32[2,256,128]{2,1,0:T(8,128)S(1)}, u32[]{:S(2)}, u32[]{:S(2)}) collective-permute-start(f32[2,256,128]{2,1,0:T(8,128)S(1)} %select_select_fusion.25), channel_id=1, source_target_pairs={{0,4},{4,0},{8,12},{12,8},{1,5},{5,1},{9,13},{13,9},{2,6},{6,2},{1... | collective-permute-start | bytes 786440 | tf_op jit(solution)/shard_map/ppermute | solution.py:200
  92.1 18.2 %collective-permute-start.32 = (f32[2,256,128]{2,1,0:T(8,128)S(1)}, f32[2,256,128]{2,1,0:T(8,128)S(1)}, u32[]{:S(2)}, u32[]{:S(2)}) collective-permute-start(f32[2,256,128]{2,1,0:T(8,128)S(1)} %select_select_fusion.9), channel_id=1, source_target_pairs={{0,4},{4,0},{8,12},{12,8},{1,5},{5,1},{9,13},{13,9},{2,6},{6,2},{1... | collective-permute-start | bytes 786440 | tf_op jit(solution)/shard_map/ppermute | solution.py:200
  97.1 13.2 %collective-permute-start.33 = (f32[2,256,128]{2,1,0:T(8,128)S(1)}, f32[2,256,128]{2,1,0:T(8,128)S(1)}, u32[]{:S(2)}, u32[]{:S(2)}) collective-permute-start(f32[2,256,128]{2,1,0:T(8,128)S(1)} %get-tuple-element.177), channel_id=1, source_target_pairs={{4,8},{8,4},{5,9},{9,5},{6,10},{10,6},{7,11},{11,7},{20,24},{24,20... | collective-permute-start | bytes 786440 | tf_op jit(solution)/shard_map/ppermute | solution.py:199
  99.4 13.5 %collective-permute-start.23 = (f32[2,256,128]{2,1,0:T(8,128)S(1)}, f32[2,256,128]{2,1,0:T(8,128)S(1)}, u32[]{:S(2)}, u32[]{:S(2)}) collective-permute-start(f32[2,256,128]{2,1,0:T(8,128)S(1)} %get-tuple-element.185), channel_id=1, source_target_pairs={{4,8},{8,4},{5,9},{9,5},{6,10},{10,6},{7,11},{11,7},{20,24},{24,20... | collective-permute-start | bytes 786440 | tf_op jit(solution)/shard_map/ppermute | solution.py:199
  100.1 12.7 %collective-permute-start.22 = (f32[2,256,128]{2,1,0:T(8,128)S(1)}, f32[2,256,128]{2,1,0:T(8,128)S(1)}, u32[]{:S(2)}, u32[]{:S(2)}) collective-permute-start(f32[2,256,128]{2,1,0:T(8,128)S(1)} %select_select_fusion.24), channel_id=1, source_target_pairs={{0,4},{4,0},{8,12},{12,8},{1,5},{5,1},{9,13},{13,9},{2,6},{6,2},{1... | collective-permute-start | bytes 786440 | tf_op jit(solution)/shard_map/ppermute | solution.py:200
  110.4 16.3 %collective-permute-start.35 = (f32[2,256,128]{2,1,0:T(8,128)S(1)}, f32[2,256,128]{2,1,0:T(8,128)S(1)}, u32[]{:S(2)}, u32[]{:S(2)}) collective-permute-start(f32[2,256,128]{2,1,0:T(8,128)S(1)} %broadcast_select_fusion.2), channel_id=1, source_target_pairs={{4,8},{8,4},{5,9},{9,5},{6,10},{10,6},{7,11},{11,7},{20,24},{24,20... | collective-permute-start | bytes 786440 | tf_op jit(solution)/shard_map/ppermute | solution.py:199
  111.1 15.6 %collective-permute-start.34 = (f32[2,256,128]{2,1,0:T(8,128)S(1)}, f32[2,256,128]{2,1,0:T(8,128)S(1)}, u32[]{:S(2)}, u32[]{:S(2)}) collective-permute-start(f32[2,256,128]{2,1,0:T(8,128)S(1)} %select_select_fusion.8), channel_id=1, source_target_pairs={{0,4},{4,0},{8,12},{12,8},{1,5},{5,1},{9,13},{13,9},{2,6},{6,2},{1... | collective-permute-start | bytes 786440 | tf_op jit(solution)/shard_map/ppermute | solution.py:200
  112.9 16.6 %collective-permute-start.25 = (f32[2,256,128]{2,1,0:T(8,128)S(1)}, f32[2,256,128]{2,1,0:T(8,128)S(1)}, u32[]{:S(2)}, u32[]{:S(2)}) collective-permute-start(f32[2,256,128]{2,1,0:T(8,128)S(1)} %broadcast_select_fusion.10), channel_id=1, source_target_pairs={{4,8},{8,4},{5,9},{9,5},{6,10},{10,6},{7,11},{11,7},{20,24},{24,20... | collective-permute-start | bytes 786440 | tf_op jit(solution)/shard_map/ppermute | solution.py:199
  113.6 15.9 %collective-permute-start.24 = (f32[2,256,128]{2,1,0:T(8,128)S(1)}, f32[2,256,128]{2,1,0:T(8,128)S(1)}, u32[]{:S(2)}, u32[]{:S(2)}) collective-permute-start(f32[2,256,128]{2,1,0:T(8,128)S(1)} %select_select_fusion.23), channel_id=1, source_target_pairs={{0,4},{4,0},{8,12},{12,8},{1,5},{5,1},{9,13},{13,9},{2,6},{6,2},{1... | collective-permute-start | bytes 786440 | tf_op jit(solution)/shard_map/ppermute | solution.py:200
  130.5 11.6 %collective-permute-start.26 = (f32[2,256,128]{2,1,0:T(8,128)S(1)}, f32[2,256,128]{2,1,0:T(8,128)S(1)}, u32[]{:S(2)}, u32[]{:S(2)}) collective-permute-start(f32[2,256,128]{2,1,0:T(8,128)S(1)} %select_select_fusion.22), channel_id=1, source_target_pairs={{0,4},{4,0},{8,12},{12,8},{1,5},{5,1},{9,13},{13,9},{2,6},{6,2},{1... | collective-permute-start | bytes 786440 | tf_op jit(solution)/shard_map/ppermute | solution.py:200
  136.5 11.2 %collective-permute-start.38 = (f32[2,256,128]{2,1,0:T(8,128)S(1)}, f32[2,256,128]{2,1,0:T(8,128)S(1)}, u32[]{:S(2)}, u32[]{:S(2)}) collective-permute-start(f32[2,256,128]{2,1,0:T(8,128)S(1)} %select_select_fusion.5), channel_id=1, source_target_pairs={{0,4},{4,0},{8,12},{12,8},{1,5},{5,1},{9,13},{13,9},{2,6},{6,2},{1... | collective-permute-start | bytes 786440 | tf_op jit(solution)/shard_map/ppermute | solution.py:200
  (55 other events, 514.2 us)
